TPU v7x, 32 devices: a whole 2x2x4 slice. The times are simulated.
32 devices in a mesh: parts: 2 (over x), pos: 8 (over z, y), slab: 2 (over core).
Axes of the slice: x: 2, y: 2, z: 4, core: 2. Of those that a mesh axis runs over, the one named last changes fastest.
Arguments:
- obj_real: float32 [8, 2048, 1024], P(('parts', 'slab'), 'pos'), parts along dimension 0, may hold values from 0.5 to 1.5
- obj_imag: float32 [8, 2048, 1024], P(('parts', 'slab'), 'pos'), parts along dimension 0, may hold values from -1.5 to 1.5
- probe: float32 [2, 256, 256], replicated, may hold values from -5 to 5
- taps: float32 [2, 63], replicated, may hold values from -1.3 to 1.3
- intensity: float32 [32, 256, 256], P(('parts', 'pos')), parts along dimension 0, may hold values from 0.25 to 8
- row_off: int32 [32], P(('parts', 'pos')), parts along dimension 0, may hold values from 0 to 255
- col_off: int32 [32], P(('parts', 'pos')), parts along dimension 0, may hold values from 0 to 768
Outputs:
- grad_real: float32 [8, 2048, 1024], P(('parts', 'slab'), 'pos'), parts along dimension 0
- grad_imag: float32 [8, 2048, 1024], P(('parts', 'slab'), 'pos'), parts along dimension 0
There are 2 independent parts, one for each index of `parts`. A program takes and returns all parts, laid end to end along the dimension named above; an argument that names none is the same for every part. Nothing has to cross between parts.
All inputs are finite; a program needn't handle non-finite values.
Results may differ from a plain program's by a relative error of at most 0.0003.
Values sent between devices are 32-bit elements; how exact they have to be, the bound alone decides.
A program may use at most 128 MiB of HBM per device.

v0:
```python
import functools
import math

import jax
import jax.numpy as jnp
import numpy as np
from jax import lax
from jax.experimental import pallas as pl
from jax.experimental.pallas import tpu as pltpu
from jax.sharding import PartitionSpec as P

F32 = jnp.float32
BF16 = jnp.bfloat16
SMEM = pl.BlockSpec(memory_space=pltpu.SMEM)
VMEM = pl.BlockSpec(memory_space=pltpu.VMEM)


def halves(x):
    high = x.astype(BF16)
    return high, (x - high.astype(F32)).astype(BF16)


def left_mul(high, low, x):
    xh, xl = halves(x)
    left = jnp.concatenate([high, high, low], 1)
    right = jnp.concatenate([xh, xl, xh], 0)
    return jnp.dot(left, right, preferred_element_type=F32)


def right_mul(x, high, low):
    xh, xl = halves(x)
    left = jnp.concatenate([xh, xl, xh], 1)
    right = jnp.concatenate([high, high, low], 0)
    return jnp.dot(left, right, preferred_element_type=F32)


def sandwich(left_h, left_l, xr, xi, right_h, right_l):
    n = xr.shape[0]
    y = left_mul(left_h, left_l, jnp.concatenate([xr, xi], 0))
    z = right_mul(jnp.concatenate([y[:n], y[n:]], 1), right_h, right_l)
    return z[:, :n], z[:, n:]


def fourier_blocks(n):
    steps = np.arange(n)
    angle = 2.0 * math.pi / n * ((steps[:, None] * steps[None, :]) % n)
    norm = 1.0 / math.sqrt(n)
    wr, wi = np.cos(angle) * norm, -np.sin(angle) * norm
    c = np.block([[wr, -wi], [wi, wr]]).astype(np.float32)
    d = np.block([[wr, wi], [-wi, wr]]).astype(np.float32)
    out = []
    for m in (c, d):
        high = m.astype(jnp.bfloat16)
        out += [high, (m - high.astype(np.float32)).astype(jnp.bfloat16)]
    return [jnp.asarray(m) for m in out]


def column_place(col, cols_all, span):
    base = jnp.minimum(col // 128 * 128, cols_all - span)
    return pl.multiple_of(base, 128), col - base


def cut_kernel(cols, obj_r, obj_i, *rest):
    outs = rest[-cols.shape[0] :]
    n = outs[0].shape[-1]
    span = n + 128
    for k, out in enumerate(outs):
        base, shift = column_place(cols[k], obj_r.shape[-1], span)
        for ri, src in enumerate((obj_r, obj_i)):
            wide = src[0, :, pl.ds(base, span)]
            out[ri, 0] = pltpu.roll(wide, lax.rem(span - shift, span), 1)[:, :n]


def wave_kernel(phase, info, *refs):
    if phase > 0:
        refs = refs[:11] + refs[12:]

    @pl.when(info[0] == phase)
    def _():
        wave_body(info, *refs)


def wave_body(
    info, own_s, own_o, halo_s, halo_o, probe, ring, intensity, ch, cl, dh, dl,
    term_s, term_o, patch, waves, ah, al, bh, bl,
):
    n = probe.shape[-1]
    depth = own_s.shape[1]
    section, row = info[0], info[1]
    unroll_by = lax.rem(n - row, n)
    from_next = lax.broadcasted_iota(jnp.int32, (n, n), 0) < row
    for own, halo, where in ((own_s, halo_s, section), (own_o, halo_o, 1 - section)):
        for d in range(depth):
            for ri in range(2):
                merged = jnp.where(from_next, halo[ri, d], own[ri, d])
                patch[where * depth + d, ri] = pltpu.roll(merged, unroll_by, 0)

    def toeplitz(k):
        rows = jnp.broadcast_to(ring[k : k + 1, :], (n, 2 * n))
        return pltpu.roll(rows, 0, 1, stride=1, stride_axis=0)[:, :n]

    for high, low, kr, ki in ((ah, al, toeplitz(0), -toeplitz(1)), (bh, bl, toeplitz(2), toeplitz(3))):
        for r0, c0, block in ((0, 0, kr), (0, n, ki), (n, 0, -ki), (n, n, kr)):
            hi, lo = halves(block)
            high[r0 : r0 + n, c0 : c0 + n] = hi
            low[r0 : r0 + n, c0 : c0 + n] = lo

    waves[0] = probe[...]
    slices = 2 * depth

    def forward(s, _):
        pr, pi = waves[s, 0], waves[s, 1]
        o_r, o_i = patch[s, 0], patch[s, 1]
        zr, zi = sandwich(
            ah[...], al[...], pr * o_r - pi * o_i, pr * o_i + pi * o_r, bh[...], bl[...]
        )
        waves[s + 1, 0] = zr
        waves[s + 1, 1] = zi
        return 0

    lax.fori_loop(0, slices, forward, 0)
    fr, fi = sandwich(
        ch[...], cl[...], waves[slices, 0], waves[slices, 1], dh[...], dl[...]
    )
    residual = 2.0 * (fr * fr + fi * fi - intensity[section])
    xr, xi = sandwich(dh[...], dl[...], residual * fr, residual * fi, ch[...], cl[...])
    waves[slices, 0] = xr
    waves[slices, 1] = xi

    def backward(t, _):
        s = slices - 1 - t
        a_r, a_i = sandwich(
            bh[...], bl[...], waves[s + 1, 0], waves[s + 1, 1], ah[...], al[...]
        )
        w_r, w_i = waves[s, 0], waves[s, 1]
        o_r, o_i = patch[s, 0], patch[s, 1]
        patch[s, 0] = a_r * w_r + a_i * w_i
        patch[s, 1] = a_i * w_r - a_r * w_i
        waves[s, 0] = a_r * o_r + a_i * o_i
        waves[s, 1] = a_i * o_r - a_r * o_i
        return 0

    lax.fori_loop(0, slices, backward, 0)
    for out, where in ((term_s, section), (term_o, 1 - section)):
        for d in range(depth):
            for ri in range(2):
                out[ri, d] = pltpu.roll(patch[where * depth + d, ri], row, 0)


def deposit_kernel(section, rows, cols, *refs):
    pieces, (out_r, out_i) = refs[:8], refs[8:]
    n = pieces[0].shape[-1]
    span = n + 128
    row_index = lax.broadcasted_iota(jnp.int32, (n, n), 0)
    first = section[0] == 0
    for ri, out in enumerate((out_r, out_i)):
        out[...] = jnp.zeros_like(out)
        for k in range(4):
            keep = row_index >= rows[k] if k < 2 else row_index < rows[k]
            term = jnp.where(first, pieces[2 * k][ri, 0], pieces[2 * k + 1][ri, 0])
            term = jnp.where(keep, term, 0.0)
            base, shift = column_place(cols[k], out.shape[-1], span)
            wide = jnp.concatenate([term, jnp.zeros((n, 128), F32)], 1)
            out[0, :, pl.ds(base, span)] += pltpu.roll(wide, shift, 1)


def local(obj_real, obj_imag, probe, taps, intensity, row_off, col_off):
    n = probe.shape[-1]
    depth, tile, cols_all = obj_real.shape
    npos, nslab = lax.axis_size("pos"), lax.axis_size("slab")
    section = lax.axis_index("slab")

    def send(x, step, routes):
        pairs = [
            (p * nslab + src, ((p + step) % npos) * nslab + dst)
            for p in range(npos)
            for src, dst in routes
        ]
        return lax.ppermute(x, ("pos", "slab"), pairs)

    given = jnp.stack([row_off, col_off])
    tile_before = send(given, 1, ((0, 0), (1, 1)))
    order = jnp.stack([section, 1 - section])
    mine, before = given[:, order], tile_before[:, order]
    rows = jnp.concatenate([mine[0], before[0]])
    cols = jnp.concatenate([mine[1], before[1]])

    window = jax.ShapeDtypeStruct((2, depth, n, n), F32)
    window_spec = pl.BlockSpec((2, 1, n, n), lambda d: (0, d, 0, 0))
    plane_spec = pl.BlockSpec((1, tile, cols_all), lambda d: (d, 0, 0))
    anywhere = pl.BlockSpec(memory_space=pl.ANY)

    def cut(places, *after):
        count = places.shape[0]
        return pl.pallas_call(
            cut_kernel,
            grid=(depth,),
            out_shape=[window] * count,
            in_specs=[SMEM, plane_spec, plane_spec] + [anywhere] * len(after),
            out_specs=[window_spec] * count,
            compiler_params=pltpu.CompilerParams(vmem_limit_bytes=40 * 2**20),
            cost_estimate=pl.CostEstimate(flops=0, bytes_accessed=8 * 2**20, transcendentals=0),
            name="cut",
        )(places, obj_real, obj_imag, *after)

    (first_halo,) = cut(tile_before[1, :1])
    halos = [[send(first_halo, -1, ((0, 0),)), send(first_halo, -1, ((1, 0),))]]
    second_halo, own_s, own_o = cut(
        jnp.concatenate([tile_before[1, 1:], mine[1]]), first_halo
    )
    halos.append([send(second_halo, -1, ((1, 1),)), send(second_halo, -1, ((0, 1),))])
    own_o = send(own_o, 0, ((0, 1), (1, 0)))

    half = (taps.shape[1] - 1) // 2
    gap = jnp.zeros((2, 2 * n - taps.shape[1]), F32)
    back = taps[:, ::-1]
    ring = jnp.concatenate(
        [
            jnp.concatenate([t[:, half:], gap, t[:, :half]], 1)
            for t in (taps, back)
        ],
        0,
    )
    info = jnp.stack([section, rows[0]]).astype(jnp.int32)
    square = pltpu.VMEM((2 * n, 2 * n), BF16)
    constants = fourier_blocks(n)

    def waves(phase, *after):
        return pl.pallas_call(
            functools.partial(wave_kernel, phase),
            out_shape=[window] * 2,
            in_specs=[SMEM] + [VMEM] * 11 + [anywhere] * len(after),
            out_specs=[VMEM] * 2,
            scratch_shapes=[
                pltpu.VMEM((2 * depth, 2, n, n), F32),
                pltpu.VMEM((2 * depth + 1, 2, n, n), F32),
                square, square, square, square,
            ],
            compiler_params=pltpu.CompilerParams(vmem_limit_bytes=48 * 2**20),
            cost_estimate=pl.CostEstimate(
                flops=(8 * depth + 4) * 24 * n**3, bytes_accessed=2**23, transcendentals=0
            ),
            name="waves",
        )(info, own_s, own_o, *halos[phase], probe, ring, intensity, *constants, *after)

    terms = [waves(0)]
    terms.append(waves(1, terms[0][0]))
    pieces = [[], [], [], []]
    for k, (same, other) in enumerate(terms):
        pieces[0].append(same)
        pieces[1].append(send(other, 0, ((k, 1 - k),)))
        pieces[2].append(send(same, 1, ((k, k),)))
        pieces[3].append(send(other, 1, ((k, 1 - k),)))
    for k in (1, 3):
        pieces[k].reverse()
    return pl.pallas_call(
        deposit_kernel,
        grid=(depth,),
        out_shape=[jax.ShapeDtypeStruct(obj_real.shape, F32)] * 2,
        in_specs=[SMEM] * 3 + [window_spec] * 8,
        out_specs=[plane_spec] * 2,
        compiler_params=pltpu.CompilerParams(vmem_limit_bytes=40 * 2**20),
        name="deposit",
    )(info[:1], rows, cols, *pieces[0], *pieces[1], *pieces[2], *pieces[3])


def solution(mesh):
    in_specs = (
        P(("parts", "slab"), "pos", None),
        P(("parts", "slab"), "pos", None),
        P(),
        P(),
        P(("parts", "pos"), None, None),
        P(("parts", "pos")),
        P(("parts", "pos")),
    )
    out_specs = (P(("parts", "slab"), "pos", None), P(("parts", "slab"), "pos", None))
    return jax.shard_map(local, mesh=mesh, in_specs=in_specs, out_specs=out_specs, check_vma=False)
```

profile of v0, /device:TPU:0, one launch (start us, length us, event | category | flops | bytes accessed | tf_op | source)
XLA Modules:
  0.0 131.5 jit_solution(4448727014400577859)
XLA Ops:
  0.6 0.7 copy.15
  1.4 0.7 copy.16
  2.1 0.1 pad_add_fusion
  2.2 3.0 %collective-permute-start = (s32[2,2]{0,1:T(2,128)S(1)}, s32[2,2]{0,1:T(2,128)S(1)}, u32[]{:S(2)}, u32[]{:S(2)}) collective-permute-start(s32[2,2]{0,1:T(2,128)S(1)} %pad_add_fusion), channel_id=1, source_target_pairs={{0,2},{1,3},{2,4},{3,5},{4,6},{5,7},{6,8},{7,9},{8,10},{9,11},{10,... | collective-permute-start | bytes 56 | tf_op jit(solution)/shard_map/ppermute | solution.py:179
  5.2 0.1 fusion
  5.2 0.6 gather_fusion
  5.8 0.2 slice_reduce_fusion.1
  6.0 3.8 %collective-permute-done = s32[2,2]{0,1:T(2,128)S(1)} collective-permute-done((s32[2,2]{0,1:T(2,128)S(1)}, s32[2,2]{0,1:T(2,128)S(1)}, u32[]{:S(2)}, u32[]{:S(2)}) %collective-permute-start) | collective-permute-done | bytes 48 | tf_op jit(solution)/shard_map/ppermute | solution.py:179
  9.7 0.6 fusion.3
  10.3 1.6 %copy-done = f32[2,256,1024]{2,1,0:T(8,128)S(1)} copy-done((f32[2,256,1024]{2,1,0:T(8,128)S(1)}, f32[2,256,1024]{2,1,0:T(8,128)}, u32[]{:S(2)}) %copy-start) | copy-done | bytes 2097176
  11.9 1.6 %copy-done.2 = f32[2,256,1024]{2,1,0:T(8,128)S(1)} copy-done((f32[2,256,1024]{2,1,0:T(8,128)S(1)}, f32[2,256,1024]{2,1,0:T(8,128)}, u32[]{:S(2)}) %copy-start.2) | copy-done | bytes 2097176
  13.5 1.5 %cut.2.rest_0_ = f32[2,2,256,256]{3,2,1,0:T(8,128)S(1)} custom-call(s32[1]{0:T(128)} %bitcast.10.cols, f32[2,256,1024]{2,1,0:T(8,128)S(1)} %copy-done, f32[2,256,1024]{2,1,0:T(8,128)S(1)} %copy-done.2), custom_call_target="tpu_custom_call" | custom-call | bytes 8388608 | tf_op jit(solution)/shard_map/cut/pallas_call | solution.py:195
  15.0 1.3 collective-permute-start.3
  16.3 3.9 %collective-permute-start.2 = (f32[2,2,256,256]{3,2,1,0:T(8,128)S(1)}, f32[2,2,256,256]{3,2,1,0:T(8,128)}, u32[]{:S(2)}, u32[]{:S(2)}) collective-permute-start(f32[2,2,256,256]{3,2,1,0:T(8,128)S(1)} %cut.2.rest_0_), channel_id=1, source_target_pairs={{0,14},{2,0},{4,2},{6,4},{8,6},{10,8},{12,10},{14,12},{16,30},{18,... | collective-permute-start | bytes 3145736 | tf_op jit(solution)/shard_map/ppermute | solution.py:179
  20.3 0.7 pad_add_fusion.4.cols
  21.0 0.0 copy-done.1
  21.0 0.0 copy-done.3
  21.0 0.0 copy-start.9
  21.0 2.9 %cut.3 = (f32[2,2,256,256]{3,2,1,0:T(8,128)}, f32[2,2,256,256]{3,2,1,0:T(8,128)S(1)}, f32[2,2,256,256]{3,2,1,0:T(8,128)S(1)}) custom-call(s32[3]{0:T(128)S(1)} %pad_add_fusion.4.cols, f32[2,256,1024]{2,1,0:T(8,128)S(1)} %copy-done.1, f32[2,256,1024]{2,1,0:T(8,128)S(1)} %copy-done.3, f32[2,2,256,256]{3,2,1,0:T(8,128)S(1)} %cut.2.rest_0_), custom_call_target="tpu_custom_call" | custom-call | bytes 8388608 | tf_op jit(solution)/shard_map/cut/pallas_call | solution.py:195
  23.9 1.0 copy-done.6
  24.9 1.4 %collective-permute-start.1 = (f32[2,2,256,256]{3,2,1,0:T(8,128)S(1)}, f32[2,2,256,256]{3,2,1,0:T(8,128)}, u32[]{:S(2)}, u32[]{:S(2)}) collective-permute-start(f32[2,2,256,256]{3,2,1,0:T(8,128)S(1)} %get-tuple-element.10), channel_id=1, source_target_pairs={{0,1},{1,0},{2,3},{3,2},{4,5},{5,4},{6,7},{7,6},{8,9},{9,8},{10,11... | collective-permute-start | bytes 3145736 | tf_op jit(solution)/shard_map/ppermute | solution.py:179
  26.3 0.5 slice.48
  26.8 0.1 fusion.2
  26.9 0.1 slice.57
  27.0 0.1 fusion.1
  27.1 0.1 slice.55
  27.1 0.7 pad_add_fusion.3.info
  27.9 0.1 maximum_maximum_fusion.refs_5_
  27.9 3.0 %collective-permute-start.5 = (f32[2,2,256,256]{3,2,1,0:T(8,128)}, f32[2,2,256,256]{3,2,1,0:T(8,128)S(1)}, u32[]{:S(2)}, u32[]{:S(2)}) collective-permute-start(f32[2,2,256,256]{3,2,1,0:T(8,128)} %get-tuple-element.12), channel_id=1, source_target_pairs={{0,15},{2,1},{4,3},{6,5},{8,7},{10,9},{12,11},{14,13},{16,31},{18,... | collective-permute-start | bytes 3145736 | tf_op jit(solution)/shard_map/ppermute | solution.py:179
  30.9 0.7 collective-permute-start.4
  31.7 8.9 %collective-permute-done.3.refs_3_ = f32[2,2,256,256]{3,2,1,0:T(8,128)} collective-permute-done((f32[2,2,256,256]{3,2,1,0:T(8,128)S(1)}, f32[2,2,256,256]{3,2,1,0:T(8,128)}, u32[]{:S(2)}, u32[]{:S(2)}) %collective-permute-start.3) | collective-permute-done | bytes 1048608 | tf_op jit(solution)/shard_map/ppermute | solution.py:179
  40.5 3.9 %collective-permute-done.2.refs_2_ = f32[2,2,256,256]{3,2,1,0:T(8,128)} collective-permute-done((f32[2,2,256,256]{3,2,1,0:T(8,128)S(1)}, f32[2,2,256,256]{3,2,1,0:T(8,128)}, u32[]{:S(2)}, u32[]{:S(2)}) %collective-permute-start.2) | collective-permute-done | bytes 1048608 | tf_op jit(solution)/shard_map/ppermute | solution.py:179
  44.4 0.0 collective-permute-done.1.refs_1_
  44.4 0.0 copy-done.9
  44.4 0.0 copy-start.11
  44.4 1.0 copy-done.11
  45.5 1.0 copy-done.13
  46.5 1.0 copy-done.14
  47.6 1.0 copy-done.15
  48.6 23.2 %waves.2 = (f32[2,2,256,256]{3,2,1,0:T(8,128)S(1)}, f32[2,2,256,256]{3,2,1,0:T(8,128)}) custom-call(s32[2]{0:T(128)S(1)} %pad_add_fusion.3.info, f32[2,2,256,256]{3,2,1,0:T(8,128)} %copy-done.6, f32[2,2,256,256]{3,2,1,0:T(8,128)} %collective-permute-done.1.refs_1_, f32[2,2,256,256]{3,2,1,0:T(8,128)} %collective-permute-done.2.refs_2_, ...), custom_call_target="tpu_custom_call" | custom-call | flops 8053063680 | bytes 8388608 | tf_op jit(solution)/shard_map/waves/pallas_call | solution.py:229
  71.9 1.3 %collective-permute-start.11 = (f32[2,2,256,256]{3,2,1,0:T(8,128)}, f32[2,2,256,256]{3,2,1,0:T(8,128)S(1)}, u32[]{:S(2)}, u32[]{:S(2)}) collective-permute-start(f32[2,2,256,256]{3,2,1,0:T(8,128)} %get-tuple-element.15), channel_id=1, source_target_pairs={{0,3},{2,5},{4,7},{6,9},{8,11},{10,13},{12,15},{14,1},{16,19},{18,... | collective-permute-start | bytes 3145736 | tf_op jit(solution)/shard_map/ppermute | solution.py:179
  73.2 1.4 %collective-permute-start.7 = (f32[2,2,256,256]{3,2,1,0:T(8,128)}, f32[2,2,256,256]{3,2,1,0:T(8,128)S(1)}, u32[]{:S(2)}, u32[]{:S(2)}) collective-permute-start(f32[2,2,256,256]{3,2,1,0:T(8,128)} %get-tuple-element.15), channel_id=1, source_target_pairs={{0,1},{2,3},{4,5},{6,7},{8,9},{10,11},{12,13},{14,15},{16,17},{18,... | collective-permute-start | bytes 3145736 | tf_op jit(solution)/shard_map/ppermute | solution.py:179
  74.6 1.9 %collective-permute-start.8 = (f32[2,2,256,256]{3,2,1,0:T(8,128)S(1)}, f32[2,2,256,256]{3,2,1,0:T(8,128)}, u32[]{:S(2)}, u32[]{:S(2)}) collective-permute-start(f32[2,2,256,256]{3,2,1,0:T(8,128)S(1)} %get-tuple-element.11.refs_11_.refs_0_), channel_id=1, source_target_pairs={{0,2},{2,4},{4,6},{6,8},{8,10},{10,12},{12,14},{14,0},{16,18},{18,... | collective-permute-start | bytes 3145736 | tf_op jit(solution)/shard_map/ppermute | solution.py:179
  76.5 0.0 collective-permute-done.5.refs_3_
  76.5 0.0 collective-permute-done.4.refs_2_
  76.5 0.0 copy-done.4
  76.5 1.0 copy-done.18
  77.5 1.0 copy-done.19
  78.5 0.0 copy-done.16
  78.5 3.8 %waves.3 = (f32[2,2,256,256]{3,2,1,0:T(8,128)}, f32[2,2,256,256]{3,2,1,0:T(8,128)}) custom-call(s32[2]{0:T(128)S(1)} %pad_add_fusion.3.info, f32[2,2,256,256]{3,2,1,0:T(8,128)} %copy-done.6, f32[2,2,256,256]{3,2,1,0:T(8,128)} %collective-permute-done.1.refs_1_, f32[2,2,256,256]{3,2,1,0:T(8,128)} %copy-done.19, f32[2,2,256,256]{3,2,1,0:T(8,128)} %copy-done.18, ...), custom_call_target="tpu_custom_call" | custom-call | flops 8053063680 | bytes 8388608 | tf_op jit(solution)/shard_map/waves/pallas_call | solution.py:229
  82.3 1.6 %collective-permute-start.9 = (f32[2,2,256,256]{3,2,1,0:T(8,128)}, f32[2,2,256,256]{3,2,1,0:T(8,128)}, u32[]{:S(2)}, u32[]{:S(2)}) collective-permute-start(f32[2,2,256,256]{3,2,1,0:T(8,128)} %get-tuple-element.13.refs_1_), channel_id=1, source_target_pairs={{1,3},{3,5},{5,7},{7,9},{9,11},{11,13},{13,15},{15,1},{17,19},{19,... | collective-permute-start | bytes 3145736 | tf_op jit(solution)/shard_map/ppermute | solution.py:179
  83.9 1.3 collective-permute-start.10
  85.2 0.6 collective-permute-done.11.refs_7_
  85.8 1.3 collective-permute-start.6
  87.1 0.6 gather_fusion.1
  87.6 0.2 slice_reduce_fusion
  87.8 0.1 pad_add_fusion.1
  87.9 0.0 collective-permute-done.7.refs_3_
  87.9 18.3 %collective-permute-done.8.refs_4_ = f32[2,2,256,256]{3,2,1,0:T(8,128)} collective-permute-done((f32[2,2,256,256]{3,2,1,0:T(8,128)S(1)}, f32[2,2,256,256]{3,2,1,0:T(8,128)}, u32[]{:S(2)}, u32[]{:S(2)}) %collective-permute-start.8) | collective-permute-done | bytes 1048608 | tf_op jit(solution)/shard_map/ppermute | solution.py:179
  106.1 0.0 collective-permute-done.9.refs_5_
  106.1 18.5 %collective-permute-done.10.refs_6_ = f32[2,2,256,256]{3,2,1,0:T(8,128)} collective-permute-done((f32[2,2,256,256]{3,2,1,0:T(8,128)}, f32[2,2,256,256]{3,2,1,0:T(8,128)}, u32[]{:S(2)}, u32[]{:S(2)}) %collective-permute-start.10) | collective-permute-done | bytes 1048608 | tf_op jit(solution)/shard_map/ppermute | solution.py:179
  124.6 0.0 collective-permute-done.6.refs_2_
  124.6 1.2 copy-done.5
  125.9 5.6 %deposit.1 = (f32[2,256,1024]{2,1,0:T(8,128)}, f32[2,256,1024]{2,1,0:T(8,128)}) custom-call(s32[1]{0:T(128)} %bitcast.section, s32[4]{0:T(128)S(1)} %get-tuple-element.26.rows, s32[4]{0:T(128)S(1)} %get-tuple-element.27.cols, f32[2,2,256,256]{3,2,1,0:T(8,128)S(1)} %copy-done.5, f32[2,2,256,256]{3,2,1,0:T(8,128)} %get-tuple-element.13.refs_1_, ...), custom_call_target="tpu_custom_call" | custom-call | tf_op jit(solution)/shard_map/deposit/pallas_call | solution.py:256
  (25 shorter events, 0.0 us)
Async XLA Ops:
  2.2 7.6 %collective-permute-start = (s32[2,2]{0,1:T(2,128)S(1)}, s32[2,2]{0,1:T(2,128)S(1)}, u32[]{:S(2)}, u32[]{:S(2)}) collective-permute-start(s32[2,2]{0,1:T(2,128)S(1)} %pad_add_fusion), channel_id=1, source_target_pairs={{0,2},{1,3},{2,4},{3,5},{4,6},{5,7},{6,8},{7,9},{8,10},{9,11},{10,... | collective-permute-start | bytes 56 | tf_op jit(solution)/shard_map/ppermute | solution.py:179
  10.3 1.6 %copy-start = (f32[2,256,1024]{2,1,0:T(8,128)S(1)}, f32[2,256,1024]{2,1,0:T(8,128)}, u32[]{:S(2)}) copy-start(f32[2,256,1024]{2,1,0:T(8,128)} %obj_r.3) | copy-start | bytes 6291460
  11.9 1.6 %copy-start.2 = (f32[2,256,1024]{2,1,0:T(8,128)S(1)}, f32[2,256,1024]{2,1,0:T(8,128)}, u32[]{:S(2)}) copy-start(f32[2,256,1024]{2,1,0:T(8,128)} %obj_i.3) | copy-start | bytes 6291460
  13.5 7.5 %copy-start.1 = (f32[2,256,1024]{2,1,0:T(8,128)S(1)}, f32[2,256,1024]{2,1,0:T(8,128)}, u32[]{:S(2)}) copy-start(f32[2,256,1024]{2,1,0:T(8,128)} %obj_r.3) | copy-start | bytes 6291460
  13.5 7.5 %copy-start.3 = (f32[2,256,1024]{2,1,0:T(8,128)S(1)}, f32[2,256,1024]{2,1,0:T(8,128)}, u32[]{:S(2)}) copy-start(f32[2,256,1024]{2,1,0:T(8,128)} %obj_i.3) | copy-start | bytes 6291460
  15.0 25.5 %collective-permute-start.3 = (f32[2,2,256,256]{3,2,1,0:T(8,128)S(1)}, f32[2,2,256,256]{3,2,1,0:T(8,128)}, u32[]{:S(2)}, u32[]{:S(2)}) collective-permute-start(f32[2,2,256,256]{3,2,1,0:T(8,128)S(1)} %cut.2.rest_0_), channel_id=1, source_target_pairs={{1,14},{3,0},{5,2},{7,4},{9,6},{11,8},{13,10},{15,12},{17,30},{19,... | collective-permute-start | bytes 3145736 | tf_op jit(solution)/shard_map/ppermute | solution.py:179
  16.3 28.1 %collective-permute-start.2 = (f32[2,2,256,256]{3,2,1,0:T(8,128)S(1)}, f32[2,2,256,256]{3,2,1,0:T(8,128)}, u32[]{:S(2)}, u32[]{:S(2)}) collective-permute-start(f32[2,2,256,256]{3,2,1,0:T(8,128)S(1)} %cut.2.rest_0_), channel_id=1, source_target_pairs={{0,14},{2,0},{4,2},{6,4},{8,6},{10,8},{12,10},{14,12},{16,30},{18,... | collective-permute-start | bytes 3145736 | tf_op jit(solution)/shard_map/ppermute | solution.py:179
  21.0 5.8 %copy-start.17 = (f32[2,63]{1,0:T(2,128)S(1)}, f32[2,63]{1,0:T(2,128)}, u32[]{:S(2)}) copy-start(f32[2,63]{1,0:T(2,128)} %param.14) | copy-start | bytes 1516
  21.0 23.4 %copy-start.7 = (f32[2,256,256]{2,1,0:T(8,128)S(1)}, f32[2,256,256]{2,1,0:T(8,128)}, u32[]{:S(2)}) copy-start(f32[2,256,256]{2,1,0:T(8,128)} %refs_4_.3) | copy-start | bytes 1572868
  21.0 23.4 %copy-start.9 = (f32[2,256,256]{2,1,0:T(8,128)S(1)}, f32[2,256,256]{2,1,0:T(8,128)}, u32[]{:S(2)}) copy-start(f32[2,256,256]{2,1,0:T(8,128)} %refs_6_.3) | copy-start | bytes 1572868
  23.9 1.0 copy-start.6
  24.9 19.6 %collective-permute-start.1 = (f32[2,2,256,256]{3,2,1,0:T(8,128)S(1)}, f32[2,2,256,256]{3,2,1,0:T(8,128)}, u32[]{:S(2)}, u32[]{:S(2)}) collective-permute-start(f32[2,2,256,256]{3,2,1,0:T(8,128)S(1)} %get-tuple-element.10), channel_id=1, source_target_pairs={{0,1},{1,0},{2,3},{3,2},{4,5},{5,4},{6,7},{7,6},{8,9},{9,8},{10,11... | collective-permute-start | bytes 3145736 | tf_op jit(solution)/shard_map/ppermute | solution.py:179
  27.9 48.6 %collective-permute-start.5 = (f32[2,2,256,256]{3,2,1,0:T(8,128)}, f32[2,2,256,256]{3,2,1,0:T(8,128)S(1)}, u32[]{:S(2)}, u32[]{:S(2)}) collective-permute-start(f32[2,2,256,256]{3,2,1,0:T(8,128)} %get-tuple-element.12), channel_id=1, source_target_pairs={{0,15},{2,1},{4,3},{6,5},{8,7},{10,9},{12,11},{14,13},{16,31},{18,... | collective-permute-start | bytes 3145736 | tf_op jit(solution)/shard_map/ppermute | solution.py:179
  30.9 45.6 %collective-permute-start.4 = (f32[2,2,256,256]{3,2,1,0:T(8,128)}, f32[2,2,256,256]{3,2,1,0:T(8,128)S(1)}, u32[]{:S(2)}, u32[]{:S(2)}) collective-permute-start(f32[2,2,256,256]{3,2,1,0:T(8,128)} %get-tuple-element.12), channel_id=1, source_target_pairs={{1,15},{3,1},{5,3},{7,5},{9,7},{11,9},{13,11},{15,13},{17,31},{19,... | collective-permute-start | bytes 3145736 | tf_op jit(solution)/shard_map/ppermute | solution.py:179
  44.4 1.0 copy-start.11
  45.5 1.0 copy-start.13
  46.5 1.0 copy-start.14
  47.6 1.0 copy-start.15
  48.6 29.9 %copy-start.8 = (f32[2,256,256]{2,1,0:T(8,128)S(1)}, f32[2,256,256]{2,1,0:T(8,128)}, u32[]{:S(2)}) copy-start(f32[2,256,256]{2,1,0:T(8,128)} %refs_4_.3) | copy-start | bytes 1572868
  48.6 29.9 %copy-start.10 = (f32[2,256,256]{2,1,0:T(8,128)S(1)}, f32[2,256,256]{2,1,0:T(8,128)}, u32[]{:S(2)}) copy-start(f32[2,256,256]{2,1,0:T(8,128)} %refs_6_.3) | copy-start | bytes 1572868
  48.6 29.9 %copy-start.12 = (bf16[512,512]{1,0:T(8,128)(2,1)S(1)}, bf16[512,512]{1,0:T(8,128)(2,1)}, u32[]{:S(2)}) copy-start(bf16[512,512]{1,0:T(8,128)(2,1)} %constant.23.clone.refs_10_) | copy-start | bytes 1572868
  48.6 29.9 %copy-start.16 = (bf16[512,512]{1,0:T(8,128)(2,1)S(1)}, bf16[512,512]{1,0:T(8,128)(2,1)}, u32[]{:S(2)}) copy-start(bf16[512,512]{1,0:T(8,128)(2,1)} %constant.20.clone.refs_7_) | copy-start | bytes 1572868
  71.9 4.7 %copy-start.4 = (f32[2,2,256,256]{3,2,1,0:T(8,128)}, f32[2,2,256,256]{3,2,1,0:T(8,128)S(1)}, u32[]{:S(2)}) copy-start(f32[2,2,256,256]{3,2,1,0:T(8,128)S(1)} %get-tuple-element.11.refs_11_.refs_0_) | copy-start | bytes 3145732
  71.9 13.9 %collective-permute-start.11 = (f32[2,2,256,256]{3,2,1,0:T(8,128)}, f32[2,2,256,256]{3,2,1,0:T(8,128)S(1)}, u32[]{:S(2)}, u32[]{:S(2)}) collective-permute-start(f32[2,2,256,256]{3,2,1,0:T(8,128)} %get-tuple-element.15), channel_id=1, source_target_pairs={{0,3},{2,5},{4,7},{6,9},{8,11},{10,13},{12,15},{14,1},{16,19},{18,... | collective-permute-start | bytes 3145736 | tf_op jit(solution)/shard_map/ppermute | solution.py:179
  73.2 14.7 %collective-permute-start.7 = (f32[2,2,256,256]{3,2,1,0:T(8,128)}, f32[2,2,256,256]{3,2,1,0:T(8,128)S(1)}, u32[]{:S(2)}, u32[]{:S(2)}) collective-permute-start(f32[2,2,256,256]{3,2,1,0:T(8,128)} %get-tuple-element.15), channel_id=1, source_target_pairs={{0,1},{2,3},{4,5},{6,7},{8,9},{10,11},{12,13},{14,15},{16,17},{18,... | collective-permute-start | bytes 3145736 | tf_op jit(solution)/shard_map/ppermute | solution.py:179
  74.6 31.6 %collective-permute-start.8 = (f32[2,2,256,256]{3,2,1,0:T(8,128)S(1)}, f32[2,2,256,256]{3,2,1,0:T(8,128)}, u32[]{:S(2)}, u32[]{:S(2)}) collective-permute-start(f32[2,2,256,256]{3,2,1,0:T(8,128)S(1)} %get-tuple-element.11.refs_11_.refs_0_), channel_id=1, source_target_pairs={{0,2},{2,4},{4,6},{6,8},{8,10},{10,12},{12,14},{14,0},{16,18},{18,... | collective-permute-start | bytes 3145736 | tf_op jit(solution)/shard_map/ppermute | solution.py:179
  76.5 1.0 copy-start.18
  77.5 1.0 copy-start.19
  82.3 23.9 %collective-permute-start.9 = (f32[2,2,256,256]{3,2,1,0:T(8,128)}, f32[2,2,256,256]{3,2,1,0:T(8,128)}, u32[]{:S(2)}, u32[]{:S(2)}) collective-permute-start(f32[2,2,256,256]{3,2,1,0:T(8,128)} %get-tuple-element.13.refs_1_), channel_id=1, source_target_pairs={{1,3},{3,5},{5,7},{7,9},{9,11},{11,13},{13,15},{15,1},{17,19},{19,... | collective-permute-start | bytes 3145736 | tf_op jit(solution)/shard_map/ppermute | solution.py:179
  83.9 40.7 %collective-permute-start.10 = (f32[2,2,256,256]{3,2,1,0:T(8,128)}, f32[2,2,256,256]{3,2,1,0:T(8,128)}, u32[]{:S(2)}, u32[]{:S(2)}) collective-permute-start(f32[2,2,256,256]{3,2,1,0:T(8,128)} %get-tuple-element.14), channel_id=1, source_target_pairs={{1,2},{3,4},{5,6},{7,8},{9,10},{11,12},{13,14},{15,0},{17,18},{19,... | collective-permute-start | bytes 3145736 | tf_op jit(solution)/shard_map/ppermute | solution.py:179
  85.8 38.9 %collective-permute-start.6 = (f32[2,2,256,256]{3,2,1,0:T(8,128)}, f32[2,2,256,256]{3,2,1,0:T(8,128)}, u32[]{:S(2)}, u32[]{:S(2)}) collective-permute-start(f32[2,2,256,256]{3,2,1,0:T(8,128)} %get-tuple-element.14), channel_id=1, source_target_pairs={{1,0},{3,2},{5,4},{7,6},{9,8},{11,10},{13,12},{15,14},{17,16},{19,... | collective-permute-start | bytes 3145736 | tf_op jit(solution)/shard_map/ppermute | solution.py:179
  124.6 1.2 copy-start.5
where the time goes:
time: 132 us
  waiting for transfers between devices  53.8 us (41%)
  Pallas kernels  37.1 us (28%)
  starting transfers between devices  22.1 us (17%)
  local copies, waits for them, and re-layouts  15.9 us (12%)
  other arithmetic  1.75 us (1%)
    ppermute x12, waiting for transfers between devices, send(): return lax.ppermute(x, ('pos', 'slab'), pairs)  53.8 us
    pallas_call x2, Pallas kernels, waves(): pl.pallas_call(functools.partial(wave_kernel, phase), out_shape=[window]...  27 us
    ppermute x12, starting transfers between devices, send(): return lax.ppermute(x, ('pos', 'slab'), pairs)  22.1 us
    unnamed x40, local copies, waits for them, and re-layouts  11.5 us
    pallas_call x1, Pallas kernels, local(): pl.pallas_call(deposit_kernel, grid=(depth,), out_shape=[jax.ShapeDtypeSt...  5.63 us
    pallas_call x2, Pallas kernels, cut(): pl.pallas_call(cut_kernel, grid=(depth,), out_shape=[window] * count, in_...  4.39 us
  transfers between devices with their start and end apart: 12, of which 6 were waited for; matrix products, arithmetic and copies ran while one was open for 3% of the time, Pallas kernels for 23%

commit v1 on v0

v1 whole, which is shorter than its diff:
```python
import functools
import math

import jax
import jax.numpy as jnp
import numpy as np
from jax import lax
from jax.experimental import pallas as pl
from jax.experimental.pallas import tpu as pltpu
from jax.sharding import PartitionSpec as P

F32 = jnp.float32
BF16 = jnp.bfloat16
SMEM = pl.BlockSpec(memory_space=pltpu.SMEM)
VMEM = pl.BlockSpec(memory_space=pltpu.VMEM)
ANY = pl.BlockSpec(memory_space=pl.ANY)
EDGE = 32
CHUNKS = 2


def halves(x):
    high = x.astype(BF16)
    return high, (x - high.astype(F32)).astype(BF16)


def left_mul(high, low, x):
    xh, xl = halves(x)
    left = jnp.concatenate([high, high, low], 1)
    right = jnp.concatenate([xh, xl, xh], 0)
    return jnp.dot(left, right, preferred_element_type=F32)


def right_mul(x, high, low):
    xh, xl = halves(x)
    left = jnp.concatenate([xh, xl, xh], 1)
    right = jnp.concatenate([high, high, low], 0)
    return jnp.dot(left, right, preferred_element_type=F32)


def fourier_left(n):
    steps = np.arange(n)
    angle = 2.0 * math.pi / n * ((steps[:, None] * steps[None, :]) % n)
    norm = 1.0 / math.sqrt(n)
    wr, wi = np.cos(angle) * norm, -np.sin(angle) * norm
    m = np.block([[wr, -wi], [wi, wr]]).astype(np.float32)
    high = m.astype(jnp.bfloat16)
    return jnp.asarray(high), jnp.asarray((m - high.astype(np.float32)).astype(jnp.bfloat16))


def column_place(col, cols_all, span):
    base = jnp.minimum(col // 128 * 128, cols_all - span)
    return pl.multiple_of(base, 128), col - base


def put(high, low, at, block):
    hi, lo = halves(block)
    high[at] = hi
    low[at] = lo


def fused_kernel(
    obj_r, obj_i, probe, ring, intensity, row_off, col_off, wh, wl,
    mine, theirs, places,
    obj_0, obj_1, patch, outbound, waves, chi, edge_out, edge_in, x_out, x_in, x_own, y_out, y_in,
    prev_row, prev_col,
    k_h, k_l, t_h, t_l, m_h, m_l, g_h, g_l, n_h, n_l, q_h, q_l, edge_m,
    sem_obj, sem_prev_s, sem_prev_r, sem_patch_s, sem_patch_r, sem_edge_s, sem_edge_r,
    sem_x_s, sem_x_r, sem_y_s, sem_y_r, sem_mine, sem_term_s, sem_term_r,
):
    n = probe.shape[-1]
    obj_v = (obj_0, obj_1)
    depth = len(obj_v)
    slices = 2 * depth
    width = n // CHUNKS
    span = n + 128
    p, q = lax.axis_index("pos"), lax.axis_index("slab")
    npos = lax.axis_size("pos")
    nxt, prv, oth = lax.rem(p + 1, npos), lax.rem(p + npos - 1, npos), 1 - q
    to_next, to_prev, to_other = {"pos": nxt}, {"pos": prv}, {"slab": oth}

    def remote(src, dst, send, recv, to):
        return pltpu.make_async_remote_copy(
            src_ref=src, dst_ref=dst, send_sem=send, recv_sem=recv,
            device_id=to, device_id_type=pl.DeviceIdType.MESH,
        )

    blocks = obj_0.shape[1]

    def obj_copies(d):
        return [
            pltpu.make_async_copy(
                src.at[d, :, pl.ds(b * 128, 128)], obj_v[d].at[ri, b], sem_obj.at[ri, d, b]
            )
            for ri, src in enumerate((obj_r, obj_i))
            for b in range(blocks)
        ]

    for d in range(depth):
        for copy in obj_copies(d):
            copy.start()

    barrier = pltpu.get_barrier_semaphore()
    for to in (to_next, to_prev, to_other):
        pl.semaphore_signal(barrier, inc=1, device_id=to, device_id_type=pl.DeviceIdType.MESH)

    def toeplitz(k):
        rows = jnp.broadcast_to(ring[k : k + 1, :], (n, 2 * n))
        return pltpu.roll(rows, 0, 1, stride=1, stride_axis=0)

    kr, ki, tr, ti = (toeplitz(k) for k in range(4))

    def embed(high, low, re, im):
        put(high, low, (slice(0, n), slice(0, n)), re)
        put(high, low, (slice(0, n), slice(n, 2 * n)), -im)
        put(high, low, (slice(n, 2 * n), slice(0, n)), im)
        put(high, low, (slice(n, 2 * n), slice(n, 2 * n)), re)

    embed(k_h, k_l, kr[:, :n], ki[:, :n])
    embed(t_h, t_l, tr[:, :n], -ti[:, :n])

    def edge_matrix(at, re, im):
        top = re + pltpu.roll(-im, EDGE, 1)
        bottom = im + pltpu.roll(re, EDGE, 1)
        both = jnp.concatenate([top, bottom], 0)
        high = both.astype(BF16).astype(F32)
        edge_m[at, :, :128] = (high + pltpu.roll(high, 2 * EDGE, 1)).astype(BF16)
        edge_m[at, :, 128:] = (both - high).astype(BF16)

    for at, re, im in ((0, kr, ki), (2, tr, -ti)):
        edge_matrix(at, re[n - EDGE :, n : n + 128], im[n - EDGE :, n : n + 128])
        edge_matrix(
            at + 1,
            pltpu.roll(re[:EDGE, 2 * n - 128 :], EDGE, 1),
            pltpu.roll(im[:EDGE, 2 * n - 128 :], EDGE, 1),
        )

    pl.semaphore_wait(barrier, 3)
    prev_copies = [
        remote(src, dst, sem_prev_s.at[k], sem_prev_r.at[k], to_next)
        for k, (src, dst) in enumerate(((row_off, prev_row), (col_off, prev_col)))
    ]
    for copy in prev_copies:
        copy.start()

    row_index = lax.broadcasted_iota(jnp.int32, (n, n), 0)

    def cut(dst, d, row, col, role):
        keep = row_index >= row if role == 0 else row_index < row
        first = jnp.minimum(col // 128, blocks - span // 128)
        shift = col - first * 128
        for ri in range(2):
            wide = jnp.concatenate([obj_v[d][ri, first + b] for b in range(span // 128)], 1)
            part = pltpu.roll(wide, lax.rem(span - shift, span), 1)[:, :n]
            dst[ri] = jnp.where(keep, part, 0.0)

    def patch_copy(role, d, owner):
        s = owner * depth + d
        return remote(
            outbound.at[role, d], patch.at[role, s],
            sem_patch_s.at[role, d], sem_patch_r.at[role, d], to_other,
        )

    def cut_role(role, rows, cols):
        for d in range(depth):
            if role == 0:
                for copy in obj_copies(d):
                    copy.wait()
            cut(outbound.at[role, d], d, rows[oth], cols[oth], role)
            patch_copy(role, d, q).start()
        for d in range(depth):
            cut(patch.at[role, q * depth + d], d, rows[q], cols[q], role)

    cut_role(0, row_off, col_off)

    row = row_off[q]
    full = left_mul(wh[...], wl[...], jnp.concatenate([kr[:, :n], ki[:, :n]], 0))
    qr, qi = full[:n], full[n:]
    put(m_h, m_l, slice(0, n), pltpu.roll(qr, row, 1))
    put(m_h, m_l, slice(n, 2 * n), pltpu.roll(qi, row, 1))
    nr, ni = qr.T, qi.T
    put(g_h, g_l, slice(0, n), pltpu.roll(nr, row, 0))
    put(g_h, g_l, slice(n, 2 * n), pltpu.roll(-ni, row, 0))
    for k in range(CHUNKS):
        c = slice(k * width, (k + 1) * width)
        put(n_h, n_l, (k, slice(0, n), slice(0, width)), nr[:, c])
        put(n_h, n_l, (k, slice(0, n), slice(width, 2 * width)), ni[:, c])
        put(n_h, n_l, (k, slice(n, 2 * n), slice(0, width)), -ni[:, c])
        put(n_h, n_l, (k, slice(n, 2 * n), slice(width, 2 * width)), nr[:, c])
        put(q_h, q_l, (k, slice(0, width), slice(0, n)), qr[c])
        put(q_h, q_l, (k, slice(0, width), slice(n, 2 * n)), -qi[c])
        put(q_h, q_l, (k, slice(width, 2 * width), slice(0, n)), qi[c])
        put(q_h, q_l, (k, slice(width, 2 * width), slice(n, 2 * n)), qr[c])

    for copy in prev_copies:
        copy.wait()
    cut_role(1, prev_row, prev_col)
    for k, src in enumerate((row_off, prev_row, col_off, prev_col)):
        places[2 * k] = src[q]
        places[2 * k + 1] = src[oth]

    for role, shift in ((0, row), (1, prev_row[q])):
        for ri in range(2):
            waves[role, 0, ri] = pltpu.roll(probe[ri], shift, 0)

    def edge_copy(step, role):
        return remote(
            edge_out.at[step, role], edge_in.at[step, role],
            sem_edge_s.at[step, role], sem_edge_r.at[step, role], (to_next, to_prev)[role],
        )

    def send_edge(step, role, z):
        at = slice(n - EDGE, n) if role == 0 else slice(0, EDGE)
        for ri in range(2):
            edge_out[step, role, ri] = z[at, ri * n : (ri + 1) * n]
        edge_copy(step, role).start()

    def add_edge(step, role, matrix, dst):
        edge_copy(step, 1 - role).wait_recv()
        x = jnp.concatenate([edge_in[step, 1 - role, 0], edge_in[step, 1 - role, 1]], 0)
        xh, xl = halves(x)
        right = jnp.concatenate([xh, xl, xh, jnp.zeros_like(xh)], 0)
        e = jnp.dot(edge_m[matrix + role], right, preferred_element_type=F32)
        at = slice(n - EDGE, n) if role == 0 else slice(0, EDGE)
        for ri in range(2):
            dst[ri, at] += e[ri * EDGE : (ri + 1) * EDGE]

    def await_patch(role, s):
        @pl.when(lax.div(s, depth) == oth)
        def _():
            patch_copy(role, lax.rem(s, depth), oth).wait_recv()

    def exit_wave(role, s):
        await_patch(role, s)
        pr, pi = waves[role, s, 0], waves[role, s, 1]
        o_r, o_i = patch[role, s, 0], patch[role, s, 1]
        return jnp.concatenate([pr * o_r - pi * o_i, pr * o_i + pi * o_r], 1)

    def stack(z):
        return jnp.concatenate([z[:, :n], z[:, n:]], 0)

    def forward(s, _):
        zs = []
        for role in range(2):
            z = right_mul(exit_wave(role, s), t_h[...], t_l[...])
            send_edge(s, role, z)
            zs.append(z)
        for role in range(2):
            y = left_mul(k_h[...], k_l[...], stack(zs[role]))
            waves[role, s + 1, 0] = y[:n]
            waves[role, s + 1, 1] = y[n:]
        for role in range(2):
            add_edge(s, role, 0, waves.at[role, s + 1])
        return 0

    lax.fori_loop(0, slices - 1, forward, 0)

    def x_copy(k):
        return remote(x_out.at[k], x_in.at[k], sem_x_s.at[k], sem_x_r.at[k], to_prev)

    def y_copy(k):
        return remote(y_out.at[k], y_in.at[k], sem_y_s.at[k], sem_y_r.at[k], to_next)

    last = slices - 1
    u = exit_wave(1, last)
    for k in range(CHUNKS):
        x_out[k] = right_mul(u, n_h[k], n_l[k])
        x_copy(k).start()
    u = exit_wave(0, last)
    for k in range(CHUNKS):
        x_own[k] = right_mul(u, n_h[k], n_l[k])

    def complex_left(high, low, x):
        w = x.shape[1] // 2
        out = left_mul(high, low, x)
        return out[:n, :w] - out[n:, w:], out[:n, w:] + out[n:, :w]

    for k in range(CHUNKS):
        x_copy(k).wait_recv()
        x = jnp.where(row_index >= row, x_own[k], x_in[k])
        fr, fi = complex_left(m_h[...], m_l[...], x)
        residual = 2.0 * (fr * fr + fi * fi - intensity[q, :, k * width : (k + 1) * width])
        g = jnp.concatenate([residual * fr, residual * fi], 1)
        yr, yi = complex_left(g_h[...], g_l[...], g)
        y_out[k] = jnp.concatenate([yr, yi], 1)
        y_copy(k).start()

    def finish(role, s, a_r, a_i):
        w_r, w_i = waves[role, s, 0], waves[role, s, 1]
        o_r, o_i = patch[role, s, 0], patch[role, s, 1]
        chi[role, 0] = a_r * o_r + a_i * o_i
        chi[role, 1] = a_i * o_r - a_r * o_i
        patch[role, s, 0] = a_r * w_r + a_i * w_i
        patch[role, s, 1] = a_i * w_r - a_r * w_i
        d = lax.rem(s, depth)
        own = lax.div(s, depth) == q

        @pl.when(own)
        def _():
            mine_copy(role, d).start()

        @pl.when(jnp.logical_not(own))
        def _():
            term_copy(role, d).start()

    def mine_copy(role, d):
        return pltpu.make_async_copy(
            patch.at[role, q * depth + d], mine.at[role, d], sem_mine.at[role, d]
        )

    def term_copy(role, d):
        return remote(
            patch.at[role, oth * depth + d], theirs.at[role, d],
            sem_term_s.at[role, d], sem_term_r.at[role, d], to_other,
        )

    for role in range(2):
        a = jnp.zeros((n, 2 * n), F32)
        for k in range(CHUNKS):
            if role == 1:
                y_copy(k).wait_recv()
            a += right_mul((y_out, y_in)[role][k], q_h[k], q_l[k])
        finish(role, last, a[:, :n], a[:, n:])

    def backward(i, _):
        s = last - 1 - i
        step = last + i
        zs = []
        for role in range(2):
            z = right_mul(
                jnp.concatenate([chi[role, 0], chi[role, 1]], 1), k_h[...], k_l[...]
            )
            send_edge(step, role, z)
            zs.append(z)
        for role in range(2):
            y = left_mul(t_h[...], t_l[...], stack(zs[role]))
            chi[role, 0] = y[:n]
            chi[role, 1] = y[n:]
        for role in range(2):
            add_edge(step, role, 2, chi.at[role])
            finish(role, s, chi[role, 0], chi[role, 1])
        return 0

    lax.fori_loop(0, slices - 1, backward, 0)

    for copy in [patch_copy(role, d, q) for role in range(2) for d in range(depth)]:
        copy.wait_send()
    for step in range(2 * (slices - 1)):
        for role in range(2):
            edge_copy(step, role).wait_send()
    for k in range(CHUNKS):
        x_copy(k).wait_send()
        y_copy(k).wait_send()
    for role in range(2):
        for d in range(depth):
            mine_copy(role, d).wait()
            term_copy(role, d).wait()


def deposit_kernel(places, mine, theirs, out_r, out_i):
    n = mine.shape[-1]
    span = n + 128
    row_index = lax.broadcasted_iota(jnp.int32, (n, n), 0)
    for ri, out in enumerate((out_r, out_i)):
        out[...] = jnp.zeros_like(out)
        for k in range(4):
            role, src = k // 2, (mine, theirs)[k % 2]
            row, col = places[k], places[4 + k]
            keep = row_index >= row if role == 0 else row_index < row
            term = jnp.where(keep, src[role, 0, ri], 0.0)
            base, shift = column_place(col, out.shape[-1], span)
            wide = jnp.concatenate([term, jnp.zeros((n, 128), F32)], 1)
            out[0, :, pl.ds(base, span)] += pltpu.roll(wide, shift, 1)


def local(obj_real, obj_imag, probe, taps, intensity, row_off, col_off):
    n = probe.shape[-1]
    depth, tile, cols_all = obj_real.shape
    slices = 2 * depth
    half = (taps.shape[1] - 1) // 2
    gap = jnp.zeros((2, 2 * n - taps.shape[1]), F32)
    back = taps[:, ::-1]
    ring = jnp.concatenate(
        [jnp.concatenate([t[:, half:], gap, t[:, :half]], 1) for t in (taps, back)], 0
    )
    wide = 2 * n // CHUNKS
    steps = 2 * (slices - 1)
    dma = pltpu.SemaphoreType.DMA
    square = pltpu.VMEM((2 * n, 2 * n), BF16)
    terms = jax.ShapeDtypeStruct((2, depth, 2, n, n), F32)
    mine, theirs, places = pl.pallas_call(
        fused_kernel,
        out_shape=[terms, terms, jax.ShapeDtypeStruct((8,), jnp.int32)],
        in_specs=[ANY, ANY, VMEM, VMEM, VMEM, SMEM, SMEM, VMEM, VMEM],
        out_specs=[ANY, ANY, SMEM],
        scratch_shapes=[
            pltpu.VMEM((2, cols_all // 128, tile, 128), F32),
            pltpu.VMEM((2, cols_all // 128, tile, 128), F32),
            pltpu.VMEM((2, slices, 2, n, n), F32),
            pltpu.VMEM((2, depth, 2, n, n), F32),
            pltpu.VMEM((2, slices, 2, n, n), F32),
            pltpu.VMEM((2, 2, n, n), F32),
            pltpu.VMEM((steps, 2, 2, EDGE, n), F32),
            pltpu.VMEM((steps, 2, 2, EDGE, n), F32),
        ]
        + [pltpu.VMEM((CHUNKS, n, wide), F32)] * 5
        + [pltpu.SMEM((2,), jnp.int32)] * 2
        + [square] * 4
        + [pltpu.VMEM((2 * n, n), BF16)] * 4
        + [pltpu.VMEM((CHUNKS, 2 * n, wide), BF16)] * 2
        + [pltpu.VMEM((CHUNKS, wide, 2 * n), BF16)] * 2
        + [pltpu.VMEM((4, 2 * EDGE, 256), BF16)]
        + [
            dma((2, depth, cols_all // 128)), dma((2,)), dma((2,)),
            dma((2, depth)), dma((2, depth)),
            dma((steps, 2)), dma((steps, 2)),
            dma((CHUNKS,)), dma((CHUNKS,)), dma((CHUNKS,)), dma((CHUNKS,)),
            dma((2, depth)), dma((2, depth)), dma((2, depth)),
        ],
        compiler_params=pltpu.CompilerParams(
            collective_id=0, has_side_effects=True, vmem_limit_bytes=56 * 2**20
        ),
        name="fused",
    )(obj_real, obj_imag, probe, ring, intensity, row_off, col_off, *fourier_left(n))

    terms_spec = pl.BlockSpec((2, 1, 2, n, n), lambda d: (0, d, 0, 0, 0))
    plane_spec = pl.BlockSpec((1, tile, cols_all), lambda d: (d, 0, 0))
    return pl.pallas_call(
        deposit_kernel,
        grid=(depth,),
        out_shape=[jax.ShapeDtypeStruct(obj_real.shape, F32)] * 2,
        in_specs=[SMEM, terms_spec, terms_spec],
        out_specs=[plane_spec] * 2,
        compiler_params=pltpu.CompilerParams(vmem_limit_bytes=40 * 2**20),
        name="deposit",
    )(places, mine, theirs)


def solution(mesh):
    in_specs = (
        P(("parts", "slab"), "pos", None),
        P(("parts", "slab"), "pos", None),
        P(),
        P(),
        P(("parts", "pos"), None, None),
        P(("parts", "pos")),
        P(("parts", "pos")),
    )
    out_specs = (P(("parts", "slab"), "pos", None), P(("parts", "slab"), "pos", None))
    return jax.shard_map(local, mesh=mesh, in_specs=in_specs, out_specs=out_specs, check_vma=False)
```

time: 132 us -> 91.8 us (0.70)
  waiting for transfers between devices: 53.8 us -> 0 us
  Pallas kernels: 37.1 us -> 84.5 us
  starting transfers between devices: 22.1 us -> 0 us
  local copies, waits for them, and re-layouts: 15.9 us -> 5.65 us
    ppermute x12 -> x0, waiting for transfers between devices: 53.8 us -> none  [send(): return lax.ppermute(x, ('pos', 'slab'), pairs)]
    pallas_call x4 -> x1, Pallas kernels: 31.4 us -> 80.3 us  [local(): pl.pallas_call(fused_kernel, out_shape=[terms, terms, jax.ShapeDtypeStruc...]
    ppermute x12 -> x0, starting transfers between devices: 22.1 us -> none  [send(): return lax.ppermute(x, ('pos', 'slab'), pairs)]
    unnamed x40 -> x6, local copies, waits for them, and re-layouts: 11.5 us -> 3.81 us
    slice x4 -> x0, local copies, waits for them, and re-layouts: 1.49 us -> none  [the longest x1 0.59 us: local(): first_halo, = cut(tile_before[1, :1])]
    another operation x2 -> x0, local copies, waits for them, and re-layouts: 1.48 us -> none  [local(): given = jnp.stack([row_off, col_off])]
    pallas_call x1, Pallas kernels: 5.63 us -> 4.22 us  [local(): pl.pallas_call(deposit_kernel, grid=(depth,), out_shape=[jax.ShapeDtypeSt...]
  transfers between devices with their start and end apart: 12 -> 0, of which waited for: 6 -> 0; matrix products, arithmetic and copies ran while one was open for 3% -> 0% of each run, Pallas kernels for 23% -> 0%
where the time goes in v1:
time: 91.8 us; the launch traced here: 91.5 us
  Pallas kernels  84.5 us (92%)
  local copies, waits for them, and re-layouts  5.65 us (6%)
    pallas_call x1, Pallas kernels, local(): pl.pallas_call(fused_kernel, out_shape=[terms, terms, jax.ShapeDtypeStruc...  80.3 us
    pallas_call x1, Pallas kernels, local(): pl.pallas_call(deposit_kernel, grid=(depth,), out_shape=[jax.ShapeDtypeSt...  4.22 us
    unnamed x6, local copies, waits for them, and re-layouts  3.81 us

profile of v1, /device:TPU:0, one launch (start us, length us, event | category | flops | bytes accessed | tf_op | source)
XLA Modules:
  0.0 91.5 jit_solution(15518059371002700305)
XLA Ops:
  0.6 0.8 fusion.1
  1.5 0.1 slice.23
  1.6 0.8 fusion
  2.4 0.1 slice.21
  2.5 0.7 maximum_maximum_fusion.ring
  3.2 80.3 %fused.1 = (f32[2,2,2,256,256]{4,3,2,1,0:T(8,128)}, f32[2,2,2,256,256]{4,3,2,1,0:T(8,128)}, s32[8]{0:T(128)}) custom-call(f32[2,256,1024]{2,1,0:T(8,128)} %obj_r.1, f32[2,256,1024]{2,1,0:T(8,128)} %obj_i.1, f32[2,256,256]{2,1,0:T(8,128)} %probe.1, f32[4,512]{1,0:T(4,128)} %maximum_maximum_fusion.ring, f32[2,256,256]{2,1,0:T(8,128)} %intensity.1, s32[2]{0:T(128)} %row_off.1, ...), custom_call_target="tpu_custom_call" | custom-call | tf_op jit(solution)/shard_map/fused/pallas_call | solution.py:390
  83.5 0.0 copy-start
  83.5 1.6 %copy-done = f32[2,2,2,256,256]{4,3,2,1,0:T(8,128)S(1)} copy-done((f32[2,2,2,256,256]{4,3,2,1,0:T(8,128)S(1)}, f32[2,2,2,256,256]{4,3,2,1,0:T(8,128)}, u32[]{:S(2)}) %copy-start) | copy-done | bytes 2097176
  85.0 0.0 copy-start.1
  85.0 1.6 %copy-done.1 = f32[2,2,2,256,256]{4,3,2,1,0:T(8,128)S(1)} copy-done((f32[2,2,2,256,256]{4,3,2,1,0:T(8,128)S(1)}, f32[2,2,2,256,256]{4,3,2,1,0:T(8,128)}, u32[]{:S(2)}) %copy-start.1) | copy-done | bytes 2097176
  86.6 0.0 copy-start.2
  86.6 0.6 copy-done.2
  87.3 4.2 %deposit.1 = (f32[2,256,1024]{2,1,0:T(8,128)}, f32[2,256,1024]{2,1,0:T(8,128)}) custom-call(s32[8]{0:T(128)S(1)} %copy-done.2, f32[2,2,2,256,256]{4,3,2,1,0:T(8,128)S(1)} %copy-done, f32[2,2,2,256,256]{4,3,2,1,0:T(8,128)S(1)} %copy-done.1), custom_call_target="tpu_custom_call" | custom-call | tf_op jit(solution)/shard_map/deposit/pallas_call | solution.py:427
  (1 shorter events, 0.0 us)
Async XLA Ops:
  83.5 1.6 %copy-start = (f32[2,2,2,256,256]{4,3,2,1,0:T(8,128)S(1)}, f32[2,2,2,256,256]{4,3,2,1,0:T(8,128)}, u32[]{:S(2)}) copy-start(f32[2,2,2,256,256]{4,3,2,1,0:T(8,128)} %get-tuple-element.6.mine) | copy-start | bytes 6291460
  85.0 1.6 %copy-start.1 = (f32[2,2,2,256,256]{4,3,2,1,0:T(8,128)S(1)}, f32[2,2,2,256,256]{4,3,2,1,0:T(8,128)}, u32[]{:S(2)}) copy-start(f32[2,2,2,256,256]{4,3,2,1,0:T(8,128)} %get-tuple-element.7.theirs) | copy-start | bytes 6291460
  86.6 0.6 copy-start.2

commit v2 on v1

v2 whole, which is shorter than its diff:
```python
import functools
import math

import jax
import jax.numpy as jnp
import numpy as np
from jax import lax
from jax.experimental import pallas as pl
from jax.experimental.pallas import tpu as pltpu
from jax.sharding import PartitionSpec as P

F32 = jnp.float32
BF16 = jnp.bfloat16
SMEM = pl.BlockSpec(memory_space=pltpu.SMEM)
VMEM = pl.BlockSpec(memory_space=pltpu.VMEM)
ANY = pl.BlockSpec(memory_space=pl.ANY)
CHUNKS = 2
EDGE = 32


def halves(x):
    high = x.astype(BF16)
    return high, (x - high.astype(F32)).astype(BF16)


def left_mul(high, low, x):
    xh, xl = halves(x)
    left = jnp.concatenate([high, high, low], 1)
    right = jnp.concatenate([xh, xl, xh], 0)
    return jnp.dot(left, right, preferred_element_type=F32)


def right_mul(x, high, low):
    xh, xl = halves(x)
    left = jnp.concatenate([xh, xl, xh], 1)
    right = jnp.concatenate([high, high, low], 0)
    return jnp.dot(left, right, preferred_element_type=F32)


def fourier_left(n):
    steps = np.arange(n)
    angle = 2.0 * math.pi / n * ((steps[:, None] * steps[None, :]) % n)
    norm = 1.0 / math.sqrt(n)
    m = np.concatenate([np.cos(angle) * norm, -np.sin(angle) * norm], 0).astype(np.float32)
    high = m.astype(jnp.bfloat16)
    return jnp.asarray(high), jnp.asarray((m - high.astype(np.float32)).astype(jnp.bfloat16))


def put(high, low, at, block):
    hi, lo = halves(block)
    high[at] = hi
    low[at] = lo


def embed(high, low, re, im):
    n = re.shape[0]
    one, two = slice(0, n), slice(n, 2 * n)
    for ref, r, i in zip((high, low), halves(re), halves(im)):
        ref[one, one] = r
        ref[one, two] = -i
        ref[two, one] = i
        ref[two, two] = r


def strip_rows(slices, half):
    forward = [half * (slices - 1 - s) for s in range(slices)]
    backward = [half * s for s in range(slices)]
    return [[-(-rows // 8) * 8 for rows in need] for need in (forward, backward)]


def fused_kernel(
    obj_r, obj_i, probe_any, taps, intensity_any, row_off, col_off, wh_any, wl_any,
    mine, theirs, places,
    obj_0, obj_1, probe, intensity, wh, wl, patch, outbound, strips, waves, chi, terms,
    x_out, x_in, x_own, y_out, y_in, ring, prev_row, prev_col,
    k_h, k_l, t_h, t_l, kb_h, kb_l, tt_h, tt_l,
    m_h, m_l, g_h, g_l, n_h, n_l, q_h, q_l, edge_out, edge_in, edge_m,
    sem_obj, sem_in, sem_prev_s, sem_prev_r, sem_patch_s, sem_patch_r, sem_strip_s, sem_strip_r,
    sem_edge_s, sem_edge_r, sem_x_s, sem_x_r, sem_y_s, sem_y_r, sem_mine, sem_term_s, sem_term_r,
):
    n = probe.shape[-1]
    obj_v = (obj_0, obj_1)
    depth = len(obj_v)
    slices = 2 * depth
    last = slices - 1
    width = n // CHUNKS
    span = n + 128
    taps_count = taps.shape[1]
    half = (taps_count - 1) // 2
    extent = strip_rows(slices, half)
    p, q = lax.axis_index("pos"), lax.axis_index("slab")
    npos = lax.axis_size("pos")
    nxt, prv, oth = lax.rem(p + 1, npos), lax.rem(p + npos - 1, npos), 1 - q

    def remote(src, dst, send, recv, pos, slab):
        return pltpu.make_async_remote_copy(
            src_ref=src, dst_ref=dst, send_sem=send, recv_sem=recv,
            device_id={"pos": pos, "slab": slab}, device_id_type=pl.DeviceIdType.MESH,
        )

    blocks = obj_0.shape[1]

    def obj_copies(d):
        return [
            pltpu.make_async_copy(
                src.at[d, :, pl.ds(b * 128, 128)], obj_v[d].at[ri, b], sem_obj.at[ri, d, b]
            )
            for ri, src in enumerate((obj_r, obj_i))
            for b in range(blocks)
        ]

    for d in range(depth):
        for copy in obj_copies(d):
            copy.start()
    small = [
        pltpu.make_async_copy(src, dst, sem_in.at[k])
        for k, (src, dst) in enumerate(
            ((wh_any, wh), (wl_any, wl), (probe_any, probe), (intensity_any.at[q], intensity))
        )
    ]
    for copy in small:
        copy.start()

    barrier = pltpu.get_barrier_semaphore()
    for pos, slab in ((nxt, q), (nxt, oth), (prv, q), (prv, oth), (p, oth)):
        pl.semaphore_signal(
            barrier, inc=1, device_id={"pos": pos, "slab": slab},
            device_id_type=pl.DeviceIdType.MESH,
        )

    row_index = lax.broadcasted_iota(jnp.int32, (n, n), 0)
    col_index = lax.broadcasted_iota(jnp.int32, (n, n), 1)
    near = jnp.abs(row_index - col_index) < n // 2

    def cut(dst, d, row, col, role):
        keep = row_index >= row if role == 0 else row_index < row
        first = jnp.minimum(col // 128, blocks - span // 128)
        shift = col - first * 128
        for ri in range(2):
            wide = jnp.concatenate([obj_v[d][ri, first + b] for b in range(span // 128)], 1)
            part = pltpu.roll(wide, lax.rem(span - shift, span), 1)[:, :n]
            dst[ri] = jnp.where(keep, part, 0.0)

    def patch_copy(role, d, owner):
        return remote(
            outbound.at[role, d], patch.at[role, owner * depth + d],
            sem_patch_s.at[role, d], sem_patch_r.at[role, d], p, oth,
        )

    def strip_copy(role, s, slab):
        rows = extent[role][s]
        at = pl.ds(n - rows, rows) if role == 0 else pl.ds(0, rows)
        src = patch.at[role, s, :, at] if slab == 0 else outbound.at[role, s % depth, :, at]
        return remote(
            src, strips.at[1 - role, s, :, pl.ds(0, rows)],
            sem_strip_s.at[role, s, slab], sem_strip_r.at[1 - role, s],
            (nxt, prv)[role], (q, oth)[slab],
        )

    group = (tuple(range(last)), tuple(range(last, 0, -1)))

    def send_strips(role):
        for s in group[role]:
            @pl.when(q == s // depth)
            def _():
                for slab in range(2):
                    strip_copy(role, s, slab).start()

    def cut_role(role, rows, cols):
        for d in range(depth):
            if role == 0:
                for copy in obj_copies(d):
                    copy.wait()
            cut(outbound.at[role, d], d, rows[oth], cols[oth], role)
            cut(patch.at[role, q * depth + d], d, rows[q], cols[q], role)

    def send_role(role):
        for d in range(depth):
            patch_copy(role, d, q).start()

    cut_role(0, row_off, col_off)
    pl.semaphore_wait(barrier, 5)
    prev_copies = [
        remote(src, dst, sem_prev_s.at[k], sem_prev_r.at[k], nxt, q)
        for k, (src, dst) in enumerate(((row_off, prev_row), (col_off, prev_col)))
    ]
    for copy in prev_copies:
        copy.start()
    send_strips(0)
    send_role(0)

    ring[...] = jnp.zeros_like(ring)
    ring[:2, :taps_count] = taps[...]
    tap = pltpu.roll(ring[...], n - half, 1)

    def circulant(k):
        rows = jnp.broadcast_to(tap[k : k + 1, :], (n, n))
        return pltpu.roll(rows, 0, 1, stride=1, stride_axis=0)

    cr, ci = circulant(0), circulant(1)
    er, ei = cr.T, -ci.T

    def masked(keep, re, im):
        return jnp.where(keep, re, 0.0), jnp.where(keep, im, 0.0)

    def cut_mask(row):
        return ((row_index < row) == (col_index < row)) == near

    def edge_matrix(at, re, im):
        top = re + pltpu.roll(-im, EDGE, 1)
        bottom = im + pltpu.roll(re, EDGE, 1)
        both = jnp.concatenate([top, bottom], 0)
        high = both.astype(BF16).astype(F32)
        edge_m[at, :, :128] = (high + pltpu.roll(high, 2 * EDGE, 1)).astype(BF16)
        edge_m[at, :, 128:] = (both - high).astype(BF16)

    def edge_copy(way, step):
        return remote(
            edge_out.at[way, step], edge_in.at[way, step],
            sem_edge_s.at[way, step], sem_edge_r.at[way, step], (prv, nxt)[way], q,
        )

    def send_edge(way, step, z):
        at = slice(0, EDGE) if way == 0 else slice(n - EDGE, n)
        for ri in range(2):
            edge_out[way, step, ri] = z[at, ri * n : (ri + 1) * n]
        edge_copy(way, step).start()

    def edge_term(way, step):
        edge_copy(way, step).wait_recv()
        xh, xl = halves(jnp.concatenate([edge_in[way, step, 0], edge_in[way, step, 1]], 0))
        right = jnp.concatenate([xh, xl, xh, jnp.zeros_like(xh)], 0)
        return jnp.dot(edge_m[way], right, preferred_element_type=F32)

    def await_patch(role, s):
        @pl.when(q != s // depth)
        def _():
            patch_copy(role, s % depth, oth).wait_recv()

    def add_strip(role, s):
        rows = extent[1 - role][s]
        at = slice(0, rows) if role == 0 else slice(n - rows, n)
        strip_copy(1 - role, s, 0).wait_recv()
        for ri in range(2):
            patch[role, s, ri, at] += strips[role, s, ri, :rows]

    def exit_wave(role, s):
        pr, pi = waves[role, s, 0], waves[role, s, 1]
        o_r, o_i = patch[role, s, 0], patch[role, s, 1]
        return jnp.concatenate([pr * o_r - pi * o_i, pr * o_i + pi * o_r], 1)

    def stack(z):
        return jnp.concatenate([z[:, :n], z[:, n:]], 0)

    def step_top(s):
        await_patch(0, s)
        z = right_mul(exit_wave(0, s), t_h[...], t_l[...])
        y = left_mul(k_h[...], k_l[...], stack(z))
        waves[0, s + 1, 0] = y[:n]
        waves[0, s + 1, 1] = y[n:]

    def edge_top(s):
        e = edge_term(0, s)
        for ri in range(2):
            waves[0, s + 1, ri, n - EDGE :] += e[ri * EDGE : (ri + 1) * EDGE]

    def step_bottom(s):
        await_patch(1, s)
        add_strip(1, s)
        z = right_mul(exit_wave(1, s), t_h[...], t_l[...])
        send_edge(0, s, z)
        y = left_mul(kb_h[...], kb_l[...], stack(z))
        waves[1, s + 1, 0] = y[:n]
        waves[1, s + 1, 1] = y[n:]

    row = row_off[q]
    kr, ki = masked(near, cr, ci)
    embed(t_h, t_l, *masked(near, er, ei))
    embed(k_h, k_l, kr, ki)
    edge_matrix(0, cr[n - EDGE :, :128], ci[n - EDGE :, :128])
    edge_matrix(
        1, pltpu.roll(er[:EDGE, n - 128 :], EDGE, 1), pltpu.roll(ei[:EDGE, n - 128 :], EDGE, 1)
    )
    for copy in small:
        copy.wait()
    for ri in range(2):
        waves[0, 0, ri] = pltpu.roll(probe[ri], row, 0)
    step_top(0)

    for copy in prev_copies:
        copy.wait()
    cut_role(1, prev_row, prev_col)
    send_role(1)
    for k, src in enumerate((row_off, prev_row, col_off, prev_col)):
        places[2 * k] = src[q]
        places[2 * k + 1] = src[oth]

    back = prev_row[q]
    embed(kb_h, kb_l, *masked(cut_mask(back), cr, ci))
    for ri in range(2):
        waves[1, 0, ri] = pltpu.roll(probe[ri], back, 0)

    def complex_left(high, low, x):
        w = x.shape[1] // 2
        out = left_mul(high, low, x)
        return out[:n, :w] - out[n:, w:], out[:n, w:] + out[n:, :w]

    qr, qi = complex_left(wh[...], wl[...], jnp.concatenate([kr, ki], 1))
    nr, ni = qr.T, qi.T
    for k in range(CHUNKS):
        c = slice(k * width, (k + 1) * width)
        put(n_h, n_l, (k, slice(0, n), slice(0, width)), nr[:, c])
        put(n_h, n_l, (k, slice(0, n), slice(width, 2 * width)), ni[:, c])
        put(n_h, n_l, (k, slice(n, 2 * n), slice(0, width)), -ni[:, c])
        put(n_h, n_l, (k, slice(n, 2 * n), slice(width, 2 * width)), nr[:, c])
        put(q_h, q_l, (k, slice(0, width), slice(0, n)), qr[c])
        put(q_h, q_l, (k, slice(0, width), slice(n, 2 * n)), -qi[c])
        put(q_h, q_l, (k, slice(width, 2 * width), slice(0, n)), qi[c])
        put(q_h, q_l, (k, slice(width, 2 * width), slice(n, 2 * n)), qr[c])

    def x_copy(k):
        return remote(x_out.at[k], x_in.at[k], sem_x_s.at[k], sem_x_r.at[k], prv, q)

    def y_copy(k):
        return remote(y_out.at[k], y_in.at[k], sem_y_s.at[k], sem_y_r.at[k], nxt, q)

    step_bottom(0)
    for s in range(1, last):
        step_bottom(s)
    await_patch(1, last)
    u = exit_wave(1, last)
    for k in range(CHUNKS):
        x_out[k] = right_mul(u, n_h[k], n_l[k])
        x_copy(k).start()
    send_strips(1)

    for s in range(1, last):
        edge_top(s - 1)
        step_top(s)
    put(m_h, m_l, slice(0, n), pltpu.roll(qr, row, 1))
    put(m_h, m_l, slice(n, 2 * n), pltpu.roll(qi, row, 1))
    put(g_h, g_l, slice(0, n), pltpu.roll(nr, row, 0))
    put(g_h, g_l, slice(n, 2 * n), pltpu.roll(-ni, row, 0))
    embed(tt_h, tt_l, *masked(cut_mask(row), er, ei))
    edge_top(last - 1)
    await_patch(0, last)
    u = exit_wave(0, last)
    for k in range(CHUNKS):
        x_own[k] = right_mul(u, n_h[k], n_l[k])

    for k in range(CHUNKS):
        x_copy(k).wait_recv()
        x = jnp.where(row_index >= row, x_own[k], x_in[k])
        fr, fi = complex_left(m_h[...], m_l[...], x)
        residual = 2.0 * (fr * fr + fi * fi - intensity[:, k * width : (k + 1) * width])
        g = jnp.concatenate([residual * fr, residual * fi], 1)
        yr, yi = complex_left(g_h[...], g_l[...], g)
        y_out[k] = jnp.concatenate([yr, yi], 1)
        y_copy(k).start()

    def mine_copy(role, d):
        return pltpu.make_async_copy(
            terms.at[role, q * depth + d], mine.at[role, d], sem_mine.at[role, d]
        )

    def term_copy(role, d):
        return remote(
            terms.at[role, oth * depth + d], theirs.at[role, d],
            sem_term_s.at[role, d], sem_term_r.at[role, d], p, oth,
        )

    def finish(role, s, a_r, a_i):
        w_r, w_i = waves[role, s, 0], waves[role, s, 1]
        terms[role, s, 0] = a_r * w_r + a_i * w_i
        terms[role, s, 1] = a_i * w_r - a_r * w_i
        if s > 0:
            o_r, o_i = patch[role, s, 0], patch[role, s, 1]
            if role == 1:
                o_r, o_i = masked(row_index < back, o_r, o_i)
            chi[role, 0] = a_r * o_r + a_i * o_i
            chi[role, 1] = a_i * o_r - a_r * o_i

        @pl.when(q == s // depth)
        def _():
            mine_copy(role, s % depth).start()

        @pl.when(q != s // depth)
        def _():
            term_copy(role, s % depth).start()

    for role in range(2):
        if role == 0:
            add_strip(0, last)
        a = jnp.zeros((n, 2 * n), F32)
        for k in range(CHUNKS):
            if role == 1:
                y_copy(k).wait_recv()
            a += right_mul((y_out, y_in)[role][k], q_h[k], q_l[k])
        finish(role, last, a[:, :n], a[:, n:])
        for s in range(last - 1, -1, -1):
            z = right_mul(
                jnp.concatenate([chi[role, 0], chi[role, 1]], 1), k_h[...], k_l[...]
            )
            if role == 0:
                send_edge(1, s, z)
                y = left_mul(tt_h[...], tt_l[...], stack(z))
                if s > 0:
                    add_strip(0, s)
            else:
                y = left_mul(t_h[...], t_l[...], stack(z))
                e = edge_term(1, s)
                y = jnp.concatenate(
                    [y[:EDGE] + e[:EDGE], y[EDGE:n], y[n : n + EDGE] + e[EDGE:], y[n + EDGE :]], 0
                )
            finish(role, s, y[:n], y[n:])

    for role in range(2):
        for d in range(depth):
            patch_copy(role, d, q).wait_send()
        for s in group[role]:
            @pl.when(q == s // depth)
            def _():
                for slab in range(2):
                    strip_copy(role, s, slab).wait_send()
        for s in range(last):
            edge_copy(role, s).wait_send()
    for k in range(CHUNKS):
        x_copy(k).wait_send()
        y_copy(k).wait_send()
    for role in range(2):
        for d in range(depth):
            mine_copy(role, d).wait()
            term_copy(role, d).wait()


def column_place(col, cols_all, span):
    base = jnp.minimum(col // 128 * 128, cols_all - span)
    return pl.multiple_of(base, 128), col - base


def deposit_kernel(places, mine, theirs, out_r, out_i):
    n = mine.shape[-1]
    span = n + 128
    row_index = lax.broadcasted_iota(jnp.int32, (n, n), 0)
    for ri, out in enumerate((out_r, out_i)):
        out[...] = jnp.zeros_like(out)
        for k in range(4):
            role, src = k // 2, (mine, theirs)[k % 2]
            row, col = places[k], places[4 + k]
            keep = row_index >= row if role == 0 else row_index < row
            term = jnp.where(keep, src[role, 0, ri], 0.0)
            base, shift = column_place(col, out.shape[-1], span)
            wide = jnp.concatenate([term, jnp.zeros((n, 128), F32)], 1)
            out[0, :, pl.ds(base, span)] += pltpu.roll(wide, shift, 1)


def local(obj_real, obj_imag, probe, taps, intensity, row_off, col_off):
    n = probe.shape[-1]
    depth, tile, cols_all = obj_real.shape
    slices = 2 * depth
    wide = 2 * n // CHUNKS
    longest = max(max(strip_rows(slices, (taps.shape[1] - 1) // 2)))
    dma = pltpu.SemaphoreType.DMA
    terms = jax.ShapeDtypeStruct((2, depth, 2, n, n), F32)
    half_obj = pltpu.VMEM((2, cols_all // 128, tile, 128), F32)
    windows = pltpu.VMEM((2, slices, 2, n, n), F32)
    mine, theirs, places = pl.pallas_call(
        fused_kernel,
        out_shape=[terms, terms, jax.ShapeDtypeStruct((8,), jnp.int32)],
        in_specs=[ANY, ANY, ANY, VMEM, ANY, SMEM, SMEM, ANY, ANY],
        out_specs=[ANY, ANY, SMEM],
        scratch_shapes=[
            half_obj, half_obj,
            pltpu.VMEM((2, n, n), F32),
            pltpu.VMEM((n, n), F32),
            pltpu.VMEM((2 * n, n), BF16),
            pltpu.VMEM((2 * n, n), BF16),
            windows,
            pltpu.VMEM((2, depth, 2, n, n), F32),
            pltpu.VMEM((2, slices, 2, longest, n), F32),
            windows,
            pltpu.VMEM((2, 2, n, n), F32),
            windows,
        ]
        + [pltpu.VMEM((CHUNKS, n, wide), F32)] * 5
        + [pltpu.VMEM((8, n), F32)]
        + [pltpu.SMEM((2,), jnp.int32)] * 2
        + [pltpu.VMEM((2 * n, 2 * n), BF16)] * 8
        + [pltpu.VMEM((2 * n, n), BF16)] * 4
        + [pltpu.VMEM((CHUNKS, 2 * n, wide), BF16)] * 2
        + [pltpu.VMEM((CHUNKS, wide, 2 * n), BF16)] * 2
        + [pltpu.VMEM((2, slices - 1, 2, EDGE, n), F32)] * 2
        + [pltpu.VMEM((2, 2 * EDGE, 8 * EDGE), BF16)]
        + [
            dma((2, depth, cols_all // 128)), dma((4,)), dma((2,)), dma((2,)),
            dma((2, depth)), dma((2, depth)), dma((2, slices, 2)), dma((2, slices)),
            dma((2, slices - 1)), dma((2, slices - 1)),
            dma((CHUNKS,)), dma((CHUNKS,)), dma((CHUNKS,)), dma((CHUNKS,)),
            dma((2, depth)), dma((2, depth)), dma((2, depth)),
        ],
        compiler_params=pltpu.CompilerParams(
            collective_id=0, has_side_effects=True, vmem_limit_bytes=60 * 2**20
        ),
        name="fused",
    )(obj_real, obj_imag, probe, taps, intensity, row_off, col_off, *fourier_left(n))

    terms_spec = pl.BlockSpec((2, 1, 2, n, n), lambda d: (0, d, 0, 0, 0))
    plane_spec = pl.BlockSpec((1, tile, cols_all), lambda d: (d, 0, 0))
    return pl.pallas_call(
        deposit_kernel,
        grid=(depth,),
        out_shape=[jax.ShapeDtypeStruct(obj_real.shape, F32)] * 2,
        in_specs=[SMEM, terms_spec, terms_spec],
        out_specs=[plane_spec] * 2,
        compiler_params=pltpu.CompilerParams(vmem_limit_bytes=60 * 2**20),
        name="deposit",
    )(places, mine, theirs)


def solution(mesh):
    in_specs = (
        P(("parts", "slab"), "pos", None),
        P(("parts", "slab"), "pos", None),
        P(),
        P(),
        P(("parts", "pos"), None, None),
        P(("parts", "pos")),
        P(("parts", "pos")),
    )
    out_specs = (P(("parts", "slab"), "pos", None), P(("parts", "slab"), "pos", None))
    return jax.shard_map(local, mesh=mesh, in_specs=in_specs, out_specs=out_specs, check_vma=False)
```

time: 91.8 us -> 78.7 us (0.86)
  Pallas kernels: 84.5 us -> 77.9 us
  local copies, waits for them, and re-layouts: 5.65 us -> 0 us
    pallas_call x1, Pallas kernels: 80.3 us -> 72.7 us  [local(): pl.pallas_call(fused_kernel, out_shape=[terms, terms, jax.ShapeDtypeStruc...]
    unnamed x6 -> x0, local copies, waits for them, and re-layouts: 3.81 us -> none
    slice x4 -> x0, local copies, waits for them, and re-layouts: 1.84 us -> none  [the longest x2 0.92 us: local(): t[:, :half]]
    pallas_call x1, Pallas kernels: 4.22 us -> 5.17 us  [local(): pl.pallas_call(deposit_kernel, grid=(depth,), out_shape=[jax.ShapeDtypeSt...]
where the time goes in v2:
time: 78.7 us; the launch traced here: 78.5 us
  Pallas kernels  77.9 us (99%)
    pallas_call x1, Pallas kernels, local(): pl.pallas_call(fused_kernel, out_shape=[terms, terms, jax.ShapeDtypeStruc...  72.7 us
    pallas_call x1, Pallas kernels, local(): pl.pallas_call(deposit_kernel, grid=(depth,), out_shape=[jax.ShapeDtypeSt...  5.17 us

profile of v2, /device:TPU:0, one launch (start us, length us, event | category | flops | bytes accessed | tf_op | source)
XLA Modules:
  0.0 78.5 jit_solution(12649405618126520772)
XLA Ops:
  0.6 72.7 %fused.1 = (f32[2,2,2,256,256]{4,3,2,1,0:T(8,128)}, f32[2,2,2,256,256]{4,3,2,1,0:T(8,128)}, s32[8]{0:T(128)}) custom-call(f32[2,256,1024]{2,1,0:T(8,128)} %obj_r.1, f32[2,256,1024]{2,1,0:T(8,128)} %obj_i.1, f32[2,256,256]{2,1,0:T(8,128)} %probe_any.1, f32[2,63]{1,0:T(2,128)} %taps.1, f32[2,256,256]{2,1,0:T(8,128)} %intensity_any.1, s32[2]{0:T(128)} %row_off.1, ...), custom_call_target="tpu_custom_call" | custom-call | tf_op jit(solution)/shard_map/fused/pallas_call | solution.py:467
  73.3 5.2 %deposit.1 = (f32[2,256,1024]{2,1,0:T(8,128)}, f32[2,256,1024]{2,1,0:T(8,128)}) custom-call(s32[8]{0:T(128)} %get-tuple-element.5.places, f32[2,2,2,256,256]{4,3,2,1,0:T(8,128)} %get-tuple-element.6.mine, f32[2,2,2,256,256]{4,3,2,1,0:T(8,128)} %get-tuple-element.7.theirs), custom_call_target="tpu_custom_call" | custom-call | tf_op jit(solution)/shard_map/deposit/pallas_call | solution.py:509

commit v3 on v2

--- a/solution.py
+++ b/solution.py
@@ -16,6 +16,7 @@
 ANY = pl.BlockSpec(memory_space=pl.ANY)
 CHUNKS = 2
 EDGE = 32
+PIECES = 2
 
 
 def halves(x):
@@ -122,7 +123,7 @@
         copy.start()
 
     barrier = pltpu.get_barrier_semaphore()
-    for pos, slab in ((nxt, q), (nxt, oth), (prv, q), (prv, oth), (p, oth)):
+    for pos, slab in ((nxt, q), (prv, q), (p, oth)):
         pl.semaphore_signal(
             barrier, inc=1, device_id={"pos": pos, "slab": slab},
             device_id_type=pl.DeviceIdType.MESH,
@@ -131,14 +132,21 @@
     row_index = lax.broadcasted_iota(jnp.int32, (n, n), 0)
     col_index = lax.broadcasted_iota(jnp.int32, (n, n), 1)
     near = jnp.abs(row_index - col_index) < n // 2
+    lane_index = lax.broadcasted_iota(jnp.int32, (n, 128), 1)
 
     def cut(dst, d, row, col, role):
         keep = row_index >= row if role == 0 else row_index < row
         first = jnp.minimum(col // 128, blocks - span // 128)
         shift = col - first * 128
+        left = lane_index < 128 - shift
         for ri in range(2):
-            wide = jnp.concatenate([obj_v[d][ri, first + b] for b in range(span // 128)], 1)
-            part = pltpu.roll(wide, lax.rem(span - shift, span), 1)[:, :n]
+            turned = [
+                pltpu.roll(obj_v[d][ri, first + b], lax.rem(128 - shift, 128), 1)
+                for b in range(span // 128)
+            ]
+            part = jnp.concatenate(
+                [jnp.where(left, a, b) for a, b in zip(turned[:-1], turned[1:])], 1
+            )
             dst[ri] = jnp.where(keep, part, 0.0)
 
     def patch_copy(role, d, owner):
@@ -147,24 +155,20 @@
             sem_patch_s.at[role, d], sem_patch_r.at[role, d], p, oth,
         )
 
-    def strip_copy(role, s, slab):
+    def strip_copy(role, s):
         rows = extent[role][s]
         at = pl.ds(n - rows, rows) if role == 0 else pl.ds(0, rows)
-        src = patch.at[role, s, :, at] if slab == 0 else outbound.at[role, s % depth, :, at]
         return remote(
-            src, strips.at[1 - role, s, :, pl.ds(0, rows)],
-            sem_strip_s.at[role, s, slab], sem_strip_r.at[1 - role, s],
-            (nxt, prv)[role], (q, oth)[slab],
-        )
+            patch.at[role, s, :, at], strips.at[1 - role, s, :, pl.ds(0, rows)],
+            sem_strip_s.at[role, s], sem_strip_r.at[1 - role, s], (nxt, prv)[role], q,
+        )
+
+    def await_patch(role, s):
+        @pl.when(q != s // depth)
+        def _():
+            patch_copy(role, s % depth, oth).wait_recv()
 
     group = (tuple(range(last)), tuple(range(last, 0, -1)))
-
-    def send_strips(role):
-        for s in group[role]:
-            @pl.when(q == s // depth)
-            def _():
-                for slab in range(2):
-                    strip_copy(role, s, slab).start()
 
     def cut_role(role, rows, cols):
         for d in range(depth):
@@ -179,15 +183,17 @@
             patch_copy(role, d, q).start()
 
     cut_role(0, row_off, col_off)
-    pl.semaphore_wait(barrier, 5)
+    pl.semaphore_wait(barrier, 3)
     prev_copies = [
         remote(src, dst, sem_prev_s.at[k], sem_prev_r.at[k], nxt, q)
         for k, (src, dst) in enumerate(((row_off, prev_row), (col_off, prev_col)))
     ]
     for copy in prev_copies:
         copy.start()
-    send_strips(0)
     send_role(0)
+    for s in group[0]:
+        await_patch(0, s)
+        strip_copy(0, s).start()
 
     ring[...] = jnp.zeros_like(ring)
     ring[:2, :taps_count] = taps[...]
@@ -232,17 +238,11 @@
         right = jnp.concatenate([xh, xl, xh, jnp.zeros_like(xh)], 0)
         return jnp.dot(edge_m[way], right, preferred_element_type=F32)
 
-    def await_patch(role, s):
-        @pl.when(q != s // depth)
-        def _():
-            patch_copy(role, s % depth, oth).wait_recv()
-
     def add_strip(role, s):
         rows = extent[1 - role][s]
-        at = slice(0, rows) if role == 0 else slice(n - rows, n)
-        strip_copy(1 - role, s, 0).wait_recv()
+        strip_copy(1 - role, s).wait_recv()
         for ri in range(2):
-            patch[role, s, ri, at] += strips[role, s, ri, :rows]
+            patch[role, s, ri, n - rows :] += strips[role, s, ri, :rows]
 
     def exit_wave(role, s):
         pr, pi = waves[role, s, 0], waves[role, s, 1]
@@ -253,7 +253,6 @@
         return jnp.concatenate([z[:, :n], z[:, n:]], 0)
 
     def step_top(s):
-        await_patch(0, s)
         z = right_mul(exit_wave(0, s), t_h[...], t_l[...])
         y = left_mul(k_h[...], k_l[...], stack(z))
         waves[0, s + 1, 0] = y[:n]
@@ -331,12 +330,15 @@
     u = exit_wave(1, last)
     for k in range(CHUNKS):
         x_out[k] = right_mul(u, n_h[k], n_l[k])
-        x_copy(k).start()
-    send_strips(1)
+        if k == 0:
+            x_copy(k).start()
 
     for s in range(1, last):
         edge_top(s - 1)
         step_top(s)
+        if s < CHUNKS:
+            x_copy(s - 1).wait_send()
+            x_copy(s).start()
     put(m_h, m_l, slice(0, n), pltpu.roll(qr, row, 1))
     put(m_h, m_l, slice(n, 2 * n), pltpu.roll(qi, row, 1))
     put(g_h, g_l, slice(0, n), pltpu.roll(nr, row, 0))
@@ -350,13 +352,17 @@
 
     for k in range(CHUNKS):
         x_copy(k).wait_recv()
-        x = jnp.where(row_index >= row, x_own[k], x_in[k])
+        x = jnp.where(row_index[:, : 2 * width] >= row, x_own[k], x_in[k])
         fr, fi = complex_left(m_h[...], m_l[...], x)
         residual = 2.0 * (fr * fr + fi * fi - intensity[:, k * width : (k + 1) * width])
         g = jnp.concatenate([residual * fr, residual * fi], 1)
         yr, yi = complex_left(g_h[...], g_l[...], g)
         y_out[k] = jnp.concatenate([yr, yi], 1)
         y_copy(k).start()
+        if k == 0:
+            x_copy(CHUNKS - 1).wait_send()
+            for s in group[1]:
+                strip_copy(1, s).start()
 
     def mine_copy(role, d):
         return pltpu.make_async_copy(
@@ -388,44 +394,45 @@
         def _():
             term_copy(role, s % depth).start()
 
+    def backward_right(x):
+        return right_mul(x, k_h[...], k_l[...])
+
     for role in range(2):
-        if role == 0:
-            add_strip(0, last)
         a = jnp.zeros((n, 2 * n), F32)
         for k in range(CHUNKS):
             if role == 1:
                 y_copy(k).wait_recv()
             a += right_mul((y_out, y_in)[role][k], q_h[k], q_l[k])
-        finish(role, last, a[:, :n], a[:, n:])
+        a_r, a_i = a[:, :n], a[:, n:]
+        finish(role, last, a_r, a_i)
         for s in range(last - 1, -1, -1):
-            z = right_mul(
-                jnp.concatenate([chi[role, 0], chi[role, 1]], 1), k_h[...], k_l[...]
-            )
+            z = backward_right(jnp.concatenate([chi[role, 0], chi[role, 1]], 1))
             if role == 0:
                 send_edge(1, s, z)
+                rows = extent[1][s + 1]
+                strip_copy(1, s + 1).wait_recv()
+                s_r, s_i = strips[0, s + 1, 0, :rows], strips[0, s + 1, 1, :rows]
+                b_r, b_i = a_r[:rows], a_i[:rows]
+                margin = jnp.concatenate([b_r * s_r + b_i * s_i, b_i * s_r - b_r * s_i], 1)
+                z = jnp.concatenate([z[:rows] + backward_right(margin), z[rows:]], 0)
                 y = left_mul(tt_h[...], tt_l[...], stack(z))
-                if s > 0:
-                    add_strip(0, s)
             else:
                 y = left_mul(t_h[...], t_l[...], stack(z))
                 e = edge_term(1, s)
                 y = jnp.concatenate(
                     [y[:EDGE] + e[:EDGE], y[EDGE:n], y[n : n + EDGE] + e[EDGE:], y[n + EDGE :]], 0
                 )
-            finish(role, s, y[:n], y[n:])
+            a_r, a_i = y[:n], y[n:]
+            finish(role, s, a_r, a_i)
 
     for role in range(2):
         for d in range(depth):
             patch_copy(role, d, q).wait_send()
         for s in group[role]:
-            @pl.when(q == s // depth)
-            def _():
-                for slab in range(2):
-                    strip_copy(role, s, slab).wait_send()
+            strip_copy(role, s).wait_send()
         for s in range(last):
             edge_copy(role, s).wait_send()
     for k in range(CHUNKS):
-        x_copy(k).wait_send()
         y_copy(k).wait_send()
     for role in range(2):
         for d in range(depth):
@@ -439,9 +446,10 @@
 
 
 def deposit_kernel(places, mine, theirs, out_r, out_i):
-    n = mine.shape[-1]
+    rows, n = mine.shape[-2:]
     span = n + 128
-    row_index = lax.broadcasted_iota(jnp.int32, (n, n), 0)
+    row_index = lax.broadcasted_iota(jnp.int32, (rows, n), 0) + pl.program_id(1) * rows
+    lane_index = lax.broadcasted_iota(jnp.int32, (rows, 128), 1)
     for ri, out in enumerate((out_r, out_i)):
         out[...] = jnp.zeros_like(out)
         for k in range(4):
@@ -450,8 +458,15 @@
             keep = row_index >= row if role == 0 else row_index < row
             term = jnp.where(keep, src[role, 0, ri], 0.0)
             base, shift = column_place(col, out.shape[-1], span)
-            wide = jnp.concatenate([term, jnp.zeros((n, 128), F32)], 1)
-            out[0, :, pl.ds(base, span)] += pltpu.roll(wide, shift, 1)
+            zero = jnp.zeros((rows, 128), F32)
+            turned = [
+                pltpu.roll(term[:, b : b + 128], lax.rem(shift, 128), 1) for b in range(0, n, 128)
+            ]
+            right = lane_index >= shift
+            wide = jnp.concatenate(
+                [jnp.where(right, a, b) for a, b in zip(turned + [zero], [zero] + turned)], 1
+            )
+            out[0, :, pl.ds(base, span)] += wide
 
 
 def local(obj_real, obj_imag, probe, taps, intensity, row_off, col_off):
@@ -493,7 +508,7 @@
         + [pltpu.VMEM((2, 2 * EDGE, 8 * EDGE), BF16)]
         + [
             dma((2, depth, cols_all // 128)), dma((4,)), dma((2,)), dma((2,)),
-            dma((2, depth)), dma((2, depth)), dma((2, slices, 2)), dma((2, slices)),
+            dma((2, depth)), dma((2, depth)), dma((2, slices)), dma((2, slices)),
             dma((2, slices - 1)), dma((2, slices - 1)),
             dma((CHUNKS,)), dma((CHUNKS,)), dma((CHUNKS,)), dma((CHUNKS,)),
             dma((2, depth)), dma((2, depth)), dma((2, depth)),
@@ -504,11 +519,11 @@
         name="fused",
     )(obj_real, obj_imag, probe, taps, intensity, row_off, col_off, *fourier_left(n))
 
-    terms_spec = pl.BlockSpec((2, 1, 2, n, n), lambda d: (0, d, 0, 0, 0))
-    plane_spec = pl.BlockSpec((1, tile, cols_all), lambda d: (d, 0, 0))
+    terms_spec = pl.BlockSpec((2, 1, 2, n // PIECES, n), lambda d, h: (0, d, 0, h, 0))
+    plane_spec = pl.BlockSpec((1, tile // PIECES, cols_all), lambda d, h: (d, h, 0))
     return pl.pallas_call(
         deposit_kernel,
-        grid=(depth,),
+        grid=(depth, PIECES),
         out_shape=[jax.ShapeDtypeStruct(obj_real.shape, F32)] * 2,
         in_specs=[SMEM, terms_spec, terms_spec],
         out_specs=[plane_spec] * 2,

time: 78.7 us -> 77.3 us (0.982)
  Pallas kernels: 77.9 us -> 76.4 us
    pallas_call x1, Pallas kernels: 72.7 us -> 71.2 us  [local(): pl.pallas_call(fused_kernel, out_shape=[terms, terms, jax.ShapeDtypeStruc...]
where the time goes in v3:
time: 77.3 us; the launch traced here: 77 us
  Pallas kernels  76.4 us (99%)
    pallas_call x1, Pallas kernels, local(): pl.pallas_call(fused_kernel, out_shape=[terms, terms, jax.ShapeDtypeStruc...  71.2 us
    pallas_call x1, Pallas kernels, local(): pl.pallas_call(deposit_kernel, grid=(depth, PIECES), out_shape=[jax.Shape...  5.17 us

profile of v3, /device:TPU:0, one launch (start us, length us, event | category | flops | bytes accessed | tf_op | source)
XLA Modules:
  0.0 77.0 jit_solution(8839014607323670809)
XLA Ops:
  0.6 71.2 %fused.1 = (f32[2,2,2,256,256]{4,3,2,1,0:T(8,128)}, f32[2,2,2,256,256]{4,3,2,1,0:T(8,128)}, s32[8]{0:T(128)}) custom-call(f32[2,256,1024]{2,1,0:T(8,128)} %obj_r.1, f32[2,256,1024]{2,1,0:T(8,128)} %obj_i.1, f32[2,256,256]{2,1,0:T(8,128)} %probe_any.1, f32[2,63]{1,0:T(2,128)} %taps.1, f32[2,256,256]{2,1,0:T(8,128)} %intensity_any.1, s32[2]{0:T(128)} %row_off.1, ...), custom_call_target="tpu_custom_call" | custom-call | tf_op jit(solution)/shard_map/fused/pallas_call | solution.py:482
  71.9 5.2 %deposit.1 = (f32[2,256,1024]{2,1,0:T(8,128)}, f32[2,256,1024]{2,1,0:T(8,128)}) custom-call(s32[8]{0:T(128)} %get-tuple-element.5.places, f32[2,2,2,256,256]{4,3,2,1,0:T(8,128)} %get-tuple-element.6.mine, f32[2,2,2,256,256]{4,3,2,1,0:T(8,128)} %get-tuple-element.7.theirs), custom_call_target="tpu_custom_call" | custom-call | tf_op jit(solution)/shard_map/deposit/pallas_call | solution.py:524

commit v4 on v3

--- a/solution.py
+++ b/solution.py
@@ -16,7 +16,7 @@
 ANY = pl.BlockSpec(memory_space=pl.ANY)
 CHUNKS = 2
 EDGE = 32
-PIECES = 2
+PIECES = 1
 
 
 def halves(x):
@@ -284,8 +284,6 @@
         copy.wait()
     for ri in range(2):
         waves[0, 0, ri] = pltpu.roll(probe[ri], row, 0)
-    step_top(0)
-
     for copy in prev_copies:
         copy.wait()
     cut_role(1, prev_row, prev_col)
@@ -316,6 +314,8 @@
         put(q_h, q_l, (k, slice(0, width), slice(n, 2 * n)), -qi[c])
         put(q_h, q_l, (k, slice(width, 2 * width), slice(0, n)), qi[c])
         put(q_h, q_l, (k, slice(width, 2 * width), slice(n, 2 * n)), qr[c])
+
+    step_top(0)
 
     def x_copy(k):
         return remote(x_out.at[k], x_in.at[k], sem_x_s.at[k], sem_x_r.at[k], prv, q)

time: 77.3 us -> 76.4 us (0.988)
  Pallas kernels: 76.4 us -> 75.6 us
where the time goes in v4:
time: 76.4 us; the launch traced here: 76.3 us
  Pallas kernels  75.6 us (99%)
    pallas_call x1, Pallas kernels, local(): pl.pallas_call(fused_kernel, out_shape=[terms, terms, jax.ShapeDtypeStruc...  71.2 us
    pallas_call x1, Pallas kernels, local(): pl.pallas_call(deposit_kernel, grid=(depth, PIECES), out_shape=[jax.Shape...  4.41 us

profile of v4, /device:TPU:0, one launch (start us, length us, event | category | flops | bytes accessed | tf_op | source)
XLA Modules:
  0.0 76.3 jit_solution(8851616774337025547)
XLA Ops:
  0.6 71.2 %fused.1 = (f32[2,2,2,256,256]{4,3,2,1,0:T(8,128)}, f32[2,2,2,256,256]{4,3,2,1,0:T(8,128)}, s32[8]{0:T(128)}) custom-call(f32[2,256,1024]{2,1,0:T(8,128)} %obj_r.1, f32[2,256,1024]{2,1,0:T(8,128)} %obj_i.1, f32[2,256,256]{2,1,0:T(8,128)} %probe_any.1, f32[2,63]{1,0:T(2,128)} %taps.1, f32[2,256,256]{2,1,0:T(8,128)} %intensity_any.1, s32[2]{0:T(128)} %row_off.1, ...), custom_call_target="tpu_custom_call" | custom-call | tf_op jit(solution)/shard_map/fused/pallas_call | solution.py:482
  71.9 4.4 %deposit.1 = (f32[2,256,1024]{2,1,0:T(8,128)}, f32[2,256,1024]{2,1,0:T(8,128)}) custom-call(s32[8]{0:T(128)} %get-tuple-element.5.places, f32[2,2,2,256,256]{4,3,2,1,0:T(8,128)} %get-tuple-element.6.mine, f32[2,2,2,256,256]{4,3,2,1,0:T(8,128)} %get-tuple-element.7.theirs), custom_call_target="tpu_custom_call" | custom-call | tf_op jit(solution)/shard_map/deposit/pallas_call | solution.py:524
